TPU v7x, 256 devices: a whole 4x4x8 slice. The times are simulated.
256 devices in a mesh: seq: 64 (over z, y, core), dp: 4 (over x).
Axes of the slice: x: 4, y: 4, z: 8, core: 2. Of those that a mesh axis runs over, the one named last changes fastest.
Arguments:
- patches: bfloat16 [4, 16384, 1280], P('dp', 'seq')
- lengths: int32 [4, 64, 4], P('dp', 'seq'), may hold values from 1 to 32, 64 in all within a row
- token_dest: int32 [4, 4096], P('dp', 'seq'), may hold values from 0 to 4095, as said below
- gain: float32 [1280], replicated, may hold values from 0.1 to 1.9
- w_qkv: bfloat16 [1280, 3840], replicated
- w_out: bfloat16 [1280, 1280], P('seq'), may hold values from -0.15625 to 0.15625
- cotangent: bfloat16 [4, 4096, 5120], P('dp', 'seq'), may hold values from -6 to 6
Outputs:
- merged: bfloat16 [4, 4096, 5120], P('dp', 'seq')
- grad_patches: bfloat16 [4, 16384, 1280], P('dp', 'seq')
- grad_out_weight: float32 [1280, 1280], P('seq')
- grad_gain: float32 [1280], P('seq')
Inputs may be any that keep to these rules, and one draw needn't show every extreme that they name: The lengths of a shard add up to 64. `token_dest`: A token of shard s that goes to shard d lands at a position from d*64 + s*1 to d*64 + (s+1) - 1, and each of these positions receives exactly one token of shard s.
All inputs are finite; a program needn't handle non-finite values.
Results may differ from a plain program's by a relative error of at most 0.01.
Values may be sent and summed in bfloat16 or wider, within the bound.
A program may use at most 128 MiB of HBM per device.

v0:
```python
import math

import jax
import jax.numpy as jnp
from jax import lax
from jax.sharding import PartitionSpec as P

HEADS = 16
GROUP = 4


eps = 1e-06


def image_mask(shard_lengths, row_count):
    image_ends = jnp.cumsum(shard_lengths * GROUP)
    row_index = jnp.arange(row_count, dtype=jnp.int32)
    image_ids = jnp.sum((row_index[:, None] >= image_ends[None, :]).astype(jnp.int32), axis=1)
    return image_ids[:, None] == image_ids[None, :]


def forward(patch_rows, shard_lengths, gain, w_qkv, w_out):
    row_count, model_width = patch_rows.shape
    head_size = model_width // HEADS
    score_scale = 1.0 / math.sqrt(head_size)
    wide_rows = patch_rows.astype(jnp.float32)
    centred = wide_rows - jnp.mean(wide_rows, axis=-1, keepdims=True)
    inv_spread = lax.rsqrt(jnp.mean(centred * centred, axis=-1, keepdims=True) + eps)
    standard = centred * inv_spread
    normed = (standard * gain).astype(jnp.bfloat16)
    projected = jnp.dot(normed, w_qkv, preferred_element_type=jnp.float32).astype(jnp.bfloat16)
    queries = projected[:, :model_width].reshape(row_count, HEADS, head_size)
    key_rows = projected[:, model_width : 2 * model_width].reshape(row_count, HEADS, head_size)
    value_rows = projected[:, 2 * model_width :].reshape(row_count, HEADS, head_size)
    scores = (
        jnp.einsum("qhe,khe->hqk", queries, key_rows, preferred_element_type=jnp.float32)
        * score_scale
    )
    same_image = image_mask(shard_lengths, row_count)
    scores = jnp.where(same_image[None], scores, -jnp.inf)
    row_max = jnp.max(scores, axis=-1, keepdims=True)
    weights_exp = jnp.exp(scores - row_max)
    probs = weights_exp / jnp.sum(weights_exp, axis=-1, keepdims=True)
    probs_low = probs.astype(jnp.bfloat16)
    attended = jnp.einsum("hqk,khe->qhe", probs_low, value_rows, preferred_element_type=jnp.float32)
    attended = attended.astype(jnp.bfloat16).reshape(row_count, model_width)
    branch = jnp.dot(attended, w_out, preferred_element_type=jnp.float32)
    block = (wide_rows + branch).astype(jnp.bfloat16)
    return (
        block,
        (standard, inv_spread, queries, key_rows, value_rows, probs, probs_low, attended),
    )


def backward(saved, block_grad, gain, w_qkv, w_out):
    standard, inv_spread, queries, key_rows, value_rows, probs, probs_low, attended = saved
    row_count, model_width = block_grad.shape
    head_size = model_width // HEADS
    score_scale = 1.0 / math.sqrt(head_size)
    incoming = block_grad.astype(jnp.float32)
    weight_grad = lax.dot_general(
        attended, block_grad, (((0,), (0,)), ((), ())), preferred_element_type=jnp.float32
    )
    grad_attended = lax.dot_general(
        block_grad, w_out, (((1,), (1,)), ((), ())), preferred_element_type=jnp.float32
    )
    grad_attended = grad_attended.astype(jnp.bfloat16).reshape(row_count, HEADS, head_size)
    grad_probs = jnp.einsum(
        "qhe,khe->hqk", grad_attended, value_rows, preferred_element_type=jnp.float32
    )
    grad_values = jnp.einsum(
        "hqk,qhe->khe", probs_low, grad_attended, preferred_element_type=jnp.float32
    ).astype(jnp.bfloat16)
    grad_scores = (
        probs * (grad_probs - jnp.sum(grad_probs * probs, axis=-1, keepdims=True)) * score_scale
    )
    grad_scores = grad_scores.astype(jnp.bfloat16)
    grad_queries = jnp.einsum(
        "hqk,khe->qhe", grad_scores, key_rows, preferred_element_type=jnp.float32
    ).astype(jnp.bfloat16)
    grad_keys = jnp.einsum(
        "hqk,qhe->khe", grad_scores, queries, preferred_element_type=jnp.float32
    ).astype(jnp.bfloat16)
    grad_projected = jnp.concatenate(
        [
            grad_queries.reshape(row_count, model_width),
            grad_keys.reshape(row_count, model_width),
            grad_values.reshape(row_count, model_width),
        ],
        axis=1,
    )
    grad_normed = lax.dot_general(
        grad_projected, w_qkv, (((1,), (1,)), ((), ())), preferred_element_type=jnp.float32
    )
    gain_grad = jnp.sum(grad_normed * standard, axis=0)
    grad_standard = grad_normed * gain
    grad_branch = inv_spread * (
        grad_standard
        - jnp.mean(grad_standard, axis=-1, keepdims=True)
        - standard * jnp.mean(grad_standard * standard, axis=-1, keepdims=True)
    )
    patch_grad = (incoming + grad_branch).astype(jnp.bfloat16)
    return (patch_grad, weight_grad, gain_grad)


def per_device(patches, lengths, token_dest, gain, w_qkv, w_out, cotangent):
    full_out = lax.all_gather(w_out, "seq", axis=0, tiled=True)
    patch_rows = patches[0]
    row_count, model_width = patch_rows.shape
    block, saved = forward(patch_rows, lengths[0, 0], gain, w_qkv, full_out)
    seq_count = lax.axis_size("seq")
    token_count = row_count // GROUP
    peer_count = token_count // seq_count
    tokens = block.reshape(token_count, GROUP * model_width)
    targets = token_dest[0]
    slot_ids = targets // token_count * peer_count + targets % peer_count
    placing = (slot_ids[:, None] == jnp.arange(token_count, dtype=jnp.int32)[None, :]).astype(
        jnp.bfloat16
    )
    outgoing = lax.dot_general(
        placing, tokens, (((0,), (0,)), ((), ())), preferred_element_type=jnp.float32
    ).astype(jnp.bfloat16)
    merged = lax.all_to_all(outgoing, "seq", split_axis=0, concat_axis=0, tiled=True)
    returned = lax.all_to_all(cotangent[0], "seq", split_axis=0, concat_axis=0, tiled=True)
    token_grad = jnp.dot(placing, returned, preferred_element_type=jnp.float32).astype(jnp.bfloat16)
    block_grad = token_grad.reshape(row_count, model_width)
    patch_grad, weight_grad, gain_grad = backward(saved, block_grad, gain, w_qkv, full_out)
    share = model_width // seq_count
    total_weight, total_gain = lax.psum((weight_grad, gain_grad), ("seq", "dp"))
    first_row = lax.axis_index("seq") * share
    own_weight = lax.dynamic_slice_in_dim(total_weight, first_row, share, 0)
    own_gain = lax.dynamic_slice_in_dim(total_gain, first_row, share, 0)
    norm_scale = 1.0 / math.sqrt(row_count * seq_count * lax.axis_size("dp"))
    return (merged[None], patch_grad[None], own_weight * norm_scale, own_gain * norm_scale)


def solution(mesh):
    placed = (
        P("dp", "seq", None),
        P("dp", "seq", None),
        P("dp", "seq"),
        P(),
        P(),
        P("seq", None),
        P("dp", "seq", None),
    )
    return jax.shard_map(
        per_device,
        mesh=mesh,
        in_specs=placed,
        out_specs=(P("dp", "seq", None), P("dp", "seq", None), P("seq", None), P("seq")),
        check_vma=False,
    )
```

profile of v0, /device:TPU:1, one launch (start us, length us, event | category | flops | bytes accessed | tf_op | source)
XLA Modules:
  0.0 469.4 jit_solution(17606625540904831600)
XLA Ops:
  8.0 0.0 copy-start.9
  8.0 0.5 broadcast.152
  8.6 2.2 reduce.2
  10.7 1.3 reshape.171
  12.0 13.2 %all-to-all-start.1 = ((bf16[64,2,2560]{2,1,0:T(2,128)(2,1)}), bf16[64,2,2560]{2,1,0:T(2,128)(2,1)S(1)}, u32[]{:S(2)}, u32[]{:S(2)}) async-start(bf16[64,2,2560]{2,1,0:T(2,128)(2,1)} %reshape.171), calls=%async_computation.1 | async-start | bytes 1310720 | tf_op jit(solution)/shard_map/all_to_all | solution.py:124
  25.2 0.0 all-reduce.2.cloned.1.call-start
  25.3 0.2 convert_reduce_fusion
  25.5 0.3 fusion.45
  25.8 6.6 %convolution_convert_fusion.2 = bf16[256,3840]{1,0:T(8,128)(2,1)S(1)} fusion(bf16[1280,3840]{1,0:T(8,128)(2,1)} %param.11, bf16[1,256,1280]{2,1,0:T(8,128)(2,1)S(1)} %copy-done, f32[1280]{0:T(1024)S(1)} %copy-done.8, f32[256]{0:T(256)S(1)} %add_rsqrt_fusion, f32[256]{0:T(256)S(1)} %broadcast_multiply_fusion.2), kind=kOutput, calls=%fused_computation.5 | convolution fusion | flops 2519203840 | bytes 12459008 | tf_op jit(solution)/shard_map/dot_general | solution.py:31
  32.4 0.1 fusion.66
  32.6 1.1 copy.52
  33.7 0.2 copy.51
  33.9 0.2 copy.50
  34.2 0.2 reduce-window.8
  34.3 0.1 convert_reduce_fusion.1
  34.4 0.1 broadcast_compare_fusion
  34.5 4.5 fusion.67
  39.1 3.5 convolution_convert_fusion.5
  42.6 3.0 all-to-all-done.1
  45.6 0.5 reshape.172
  46.1 0.4 convolution_convert_fusion
  46.5 0.4 reshape.162
  46.9 4.8 %fusion.69 = f32[1280,1280]{1,0:T(8,128)} fusion(bf16[256,1280]{0,1:T(8,128)(2,1)} %bitcast.99, bf16[256,1280]{1,0:T(8,128)(2,1)S(1)} %reshape.162), kind=kOutput, calls=%fused_computation.89 | convolution fusion | flops 838860800 | bytes 7864320 | tf_op jit(solution)/shard_map/dot_general | solution.py:61
  51.7 0.0 all-reduce.2.cloned.1.call-update
  51.7 0.2 all-gather.3.cloned.1.call-start
  52.0 0.3 all-gather.3.cloned.1.call-update
  52.3 273.0 %all-reduce.2.cloned.1.call-done = f32[1280,1280]{1,0:T(8,128)} async-done(((f32[1280,1280]{1,0:T(8,128)}), f32[1280,1280]{1,0:T(8,128)}) %all-reduce.2.cloned.1.call-update) | async-done | bytes 6553616 | tf_op jit(solution)/shard_map/psum | solution.py:129
  325.3 1.6 dynamic-slice_multiply_fusion
  326.9 6.1 %reshape.168 = bf16[1280,1280]{1,0:T(8,128)(2,1)} reshape(bf16[64,20,1280]{2,1,0:T(8,128)(2,1)} %all-gather.3.cloned.1.call-done) | data formatting | bytes 6553600
  333.0 3.1 convolution_convert_fusion.3
  336.2 1.0 fusion.7
  337.2 0.2 copy.56
  337.5 3.9 convolution_convert_fusion.4
  341.3 2.7 fusion.68
  344.0 8.2 %fusion.32 = bf16[16,80,256]{2,1,0:T(8,128)(2,1)} fusion(bf16[256,16,80]{0,2,1:T(8,128)(2,1)S(1)} %bitcast.103, f32[16,256,256]{1,2,0:T(8,128)} %fusion.68, f32[16,256,256]{1,2,0:T(8,128)} %get-tuple-element.11, f32[16,256]{1,0:T(8,128)S(1)} %get-tuple-element.10), kind=kOutput, calls=%fused_computation.38 | convolution fusion | flops 175444224 | bytes 9715712 | tf_op jit(solution)/shard_map/hqk,khe->qhe/dot_general | solution.py:78
  352.2 8.0 %fusion.35 = bf16[16,80,256]{2,1,0:T(8,128)(2,1)} fusion(bf16[256,16,80]{0,2,1:T(8,128)(2,1)S(1)} %bitcast.105, f32[16,256,256]{1,2,0:T(8,128)} %fusion.68, f32[16,256,256]{1,2,0:T(8,128)} %get-tuple-element.11, f32[16,256]{1,0:T(8,128)S(1)} %get-tuple-element.10), kind=kOutput, calls=%fused_computation.39 | convolution fusion | flops 175444224 | bytes 9715712 | tf_op jit(solution)/shard_map/hqk,qhe->khe/dot_general | solution.py:81
  360.2 0.4 reshape.161
  360.6 0.5 fusion.2
  361.1 1.1 reduce.1
  362.2 1.3 reshape.169
  363.5 10.7 %all-to-all-start = ((bf16[64,2,2560]{2,1,0:T(2,128)(2,1)}), bf16[64,2,2560]{2,1,0:T(2,128)(2,1)S(1)}, u32[]{:S(2)}, u32[]{:S(2)}) async-start(bf16[64,2,2560]{2,1,0:T(2,128)(2,1)} %reshape.169), calls=%async_computation | async-start | bytes 1310720 | tf_op jit(solution)/shard_map/all_to_all | solution.py:123
  374.2 7.5 %fusion.44 = (f32[1280]{0:T(1024)S(1)}, f32[256]{0:T(256)S(1)}, f32[256]{0:T(256)S(1)}, f32[256,1280]{1,0:T(8,128)S(1)}) fusion(bf16[1,256,1280]{2,1,0:T(8,128)(2,1)S(1)} %copy-done, f32[256]{0:T(256)S(1)} %add_rsqrt_fusion, f32[256]{0:T(256)S(1)} %broadcast_multiply_fusion.2, f32[1280]{0:T(1024)S(1)} %copy-done.8, bf16[1280,3840]{1,0:T(8,128)(2,1)} %param.11, ...), kind=kOutput, calls=%fused_computation.48 | convolution fusion | flops 2525427968 | bytes 13776896 | tf_op jit(solution)/shard_map/dot_general | solution.py:92
  381.7 76.7 %psum.15 = f32[1280]{0:T(1024)S(1)} all-reduce(f32[1280]{0:T(1024)S(1)} %get-tuple-element.4), channel_id=1, replica_groups=mesh['seq'=64,'dp'=4] {'seq','dp'}, use_global_device_ids=true, to_apply=%region_11.12 | all-reduce | flops 1280 | bytes 10240 | tf_op jit(solution)/shard_map/psum | solution.py:129
  458.4 0.6 dynamic-slice_multiply_fusion.1
  459.0 1.4 fusion.48
  460.4 0.0 all-to-all-done
  460.4 0.5 reshape.170
  460.9 1.0 copy.71
  (27 shorter events, 0.1 us)
Async XLA Ops:
  8.0 17.2 %copy-start.9 = (s32[1,64]{1,0:T(1,128)S(1)}, s32[1,64]{1,0:T(1,128)}, u32[]{:S(2)}) copy-start(s32[1,64]{1,0:T(1,128)} %param.9) | copy-start | bytes 772
  8.0 17.3 %copy-start.10 = (s32[1,1,4]{2,1,0:T(1,128)S(1)}, s32[1,1,4]{2,1,0:T(1,128)}, u32[]{:S(2)}) copy-start(s32[1,1,4]{2,1,0:T(1,128)} %param.8) | copy-start | bytes 52
  8.0 17.3 %copy-start = (bf16[1,256,1280]{2,1,0:T(8,128)(2,1)S(1)}, bf16[1,256,1280]{2,1,0:T(8,128)(2,1)}, u32[]{:S(2)}) copy-start(bf16[1,256,1280]{2,1,0:T(8,128)(2,1)} %param.7) | copy-start | bytes 1966084
  8.0 17.8 %copy-start.8 = (f32[1280]{0:T(1024)S(1)}, f32[1280]{0:T(1024)}, u32[]{:S(2)}) copy-start(f32[1280]{0:T(1024)} %param.10) | copy-start | bytes 15364
  12.0 33.5 %all-to-all-start.1 = ((bf16[64,2,2560]{2,1,0:T(2,128)(2,1)}), bf16[64,2,2560]{2,1,0:T(2,128)(2,1)S(1)}, u32[]{:S(2)}, u32[]{:S(2)}) async-start(bf16[64,2,2560]{2,1,0:T(2,128)(2,1)} %reshape.171), calls=%async_computation.1 | async-start | bytes 1310720 | tf_op jit(solution)/shard_map/all_to_all | solution.py:124
  25.2 300.1 %all-reduce.2.cloned.1.call-start = ((), (), s32[]{:S(2)}) async-start(), calls=%async_computation.2 | async-start | bytes 13107200 | tf_op jit(solution)/shard_map/psum | solution.py:129
  33.9 5.2 %copy-start.6 = (bf16[256,1280]{0,1:T(8,128)(2,1)}, bf16[256,1280]{0,1:T(8,128)(2,1)S(1)}, u32[]{:S(2)}) copy-start(bf16[256,1280]{0,1:T(8,128)(2,1)S(1)} %copy.51) | copy-start | bytes 1966084
  34.1 4.9 %copy-start.2 = (bf16[256,1280]{0,1:T(8,128)(2,1)}, bf16[256,1280]{0,1:T(8,128)(2,1)S(1)}, u32[]{:S(2)}) copy-start(bf16[256,1280]{0,1:T(8,128)(2,1)S(1)} %copy.50) | copy-start | bytes 1966084
  51.7 275.2 %all-gather.3.cloned.1.call-start = ((), (), s32[]{:S(2)}) async-start(), calls=%async_computation.3 | async-start | bytes 3993600 | tf_op jit(solution)/shard_map/all_gather | solution.py:107
  333.0 3.1 copy-start.1
  333.0 3.1 copy-start.4
  337.5 3.9 copy-start.3
  341.3 2.7 copy-start.5
  344.0 8.2 %copy-start.7 = (bf16[256,1280]{0,1:T(8,128)(2,1)S(1)}, bf16[256,1280]{0,1:T(8,128)(2,1)}, u32[]{:S(2)}) copy-start(bf16[256,1280]{0,1:T(8,128)(2,1)} %copy-done.6) | copy-start | bytes 1966084
  363.5 96.9 %all-to-all-start = ((bf16[64,2,2560]{2,1,0:T(2,128)(2,1)}), bf16[64,2,2560]{2,1,0:T(2,128)(2,1)S(1)}, u32[]{:S(2)}, u32[]{:S(2)}) async-start(bf16[64,2,2560]{2,1,0:T(2,128)(2,1)} %reshape.169), calls=%async_computation | async-start | bytes 1310720 | tf_op jit(solution)/shard_map/all_to_all | solution.py:123
Sparse Core Ops, SparseCore 0:
  51.8 273.4 all-reduce.1
Sparse Core Ops, SparseCore 1:
  54.9 77.7 all-gather.2
where the time goes:
time: 470 us; the launch traced here: 469 us
  waiting for transfers between devices  276 us (59%)
  blocking collectives  76.7 us (16%)
  matrix products  54.7 us (12%)
  starting transfers between devices  24.2 us (5%)
  between operations  15.7 us (3%)
  local copies, waits for them, and re-layouts  14.1 us (3%)
  other arithmetic  7.71 us (2%)
    psum x1, waiting for transfers between devices, per_device(): total_weight, total_gain = lax.psum((weight_grad, gain_grad), ('seq', 'dp'))  273 us
    psum x1, blocking collectives, per_device(): total_weight, total_gain = lax.psum((weight_grad, gain_grad), ('seq', 'dp'))  76.7 us
    all_to_all x1, starting transfers between devices, per_device(): lax.all_to_all(cotangent[0], 'seq', split_axis=0, concat_axis=0, tiled=True)  13.2 us
    unnamed x28, local copies, waits for them, and re-layouts  10.9 us
    all_to_all x1, starting transfers between devices, per_device(): lax.all_to_all(outgoing, 'seq', split_axis=0, concat_axis=0, tiled=True)  10.7 us
  transfers between devices with their start and end apart: 4, of which 2 were waited for; matrix products, arithmetic and copies ran while one was open for 6% of the time, Pallas kernels for 0%

commit v1 on v0

--- a/solution.py
+++ b/solution.py
@@ -3,13 +3,348 @@
 import jax
 import jax.numpy as jnp
 from jax import lax
+from jax.experimental import pallas as pl
+from jax.experimental.pallas import tpu as pltpu
 from jax.sharding import PartitionSpec as P
 
 HEADS = 16
 GROUP = 4
-
+D = 1280
+HALF = 640
+NZ, NY, NX = 8, 4, 4
+SEQ = 64
+LIMIT = 56 * 2**20
 
 eps = 1e-06
+F32 = jnp.float32
+BF16 = jnp.bfloat16
+
+
+def place():
+    seq = lax.axis_index("seq")
+    x = lax.axis_index("dp")
+    return seq, x, lax.div(seq, 8), lax.rem(lax.div(seq, 2), 4), lax.rem(seq, 2)
+
+
+def seq_of(z, y, core):
+    return z * 8 + y * 2 + core
+
+
+def dev(seq, x):
+    return {"seq": seq, "dp": x}
+
+
+def remote(src, dst, send, recv, seq, x):
+    return pltpu.make_async_remote_copy(
+        src_ref=src,
+        dst_ref=dst,
+        send_sem=send,
+        recv_sem=recv,
+        device_id=dev(seq, x),
+        device_id_type=pl.DeviceIdType.MESH,
+    )
+
+
+def greet(with_xy):
+    seq, x, z, y, core = place()
+    barrier = pltpu.get_barrier_semaphore()
+
+    @pl.loop(1, SEQ)
+    def _(k):
+        pl.semaphore_signal(
+            barrier, inc=1, device_id=dev(lax.rem(seq + k, SEQ), x), device_id_type=pl.DeviceIdType.MESH
+        )
+
+    count = SEQ - 1
+    if with_xy:
+        for kx in range(1, NX):
+            for ky in range(NY):
+                pl.semaphore_signal(
+                    barrier,
+                    inc=1,
+                    device_id=dev(seq_of(z, lax.rem(y + ky, NY), core), lax.rem(x + kx, NX)),
+                    device_id_type=pl.DeviceIdType.MESH,
+                )
+                count += 1
+    pl.semaphore_wait(barrier, count)
+
+
+def exchange_start(src, dst, send, recv):
+    seq, x, z, y, core = place()
+
+    @pl.loop(1, SEQ)
+    def _(k):
+        to = lax.rem(seq + k, SEQ)
+        remote(src.at[to], dst.at[seq], send, recv, to, x).start()
+
+    pltpu.make_async_copy(src.at[seq], dst.at[seq], recv).start()
+
+
+def exchange_wait(src, dst, send, recv):
+    pltpu.make_async_copy(dst, dst, recv).wait()
+    part = src.at[pl.ds(0, SEQ - 1)]
+    pltpu.make_async_copy(part, part, send).wait()
+
+
+def pick(rows, columns, first):
+    r = lax.broadcasted_iota(jnp.int32, (rows, columns), 0)
+    c = lax.broadcasted_iota(jnp.int32, (rows, columns), 1)
+    return r, c
+
+
+def gather_out_weight(w_ref, slots, wg, sems):
+    seq, x, z, y, core = place()
+    own = jnp.concatenate([w_ref[...].astype(F32), jnp.zeros((12, D), F32)], axis=0).astype(BF16)
+    slots[core] = own
+    pair = remote(slots.at[core], slots.at[core], sems.at[0], sems.at[1], seq_of(z, y, 1 - core), x)
+    pair.start()
+    pair.wait()
+    r, c = pick(48, 64, 0)
+    want = jnp.where(r < 20, r, r + 12)
+    chosen = jnp.where((c == want) & (r < 40), 1.0, 0.0).astype(BF16)
+    first = pl.multiple_of(core * HALF, 128)
+    rows = jnp.concatenate([slots[0, :, pl.ds(first, HALF)], slots[1, :, pl.ds(first, HALF)]], axis=0)
+    wg[core, z, y] = jnp.dot(chosen, rows, preferred_element_type=F32).astype(BF16)
+    copies = []
+    for k in range(1, NZ):
+        copies.append(
+            remote(
+                wg.at[core, z, y], wg.at[core, z, y], sems.at[2 * k], sems.at[2 * k + 1],
+                seq_of(lax.rem(z + k, NZ), y, core), x,
+            )
+        )
+    for one in copies:
+        one.start()
+    for one in copies:
+        one.wait()
+    copies = []
+    for k in range(1, NY):
+        copies.append(
+            remote(
+                wg.at[core, :, y], wg.at[core, :, y], sems.at[14 + 2 * k], sems.at[15 + 2 * k],
+                seq_of(z, lax.rem(y + k, NY), core), x,
+            )
+        )
+    for one in copies:
+        one.start()
+    for one in copies:
+        one.wait()
+    last = remote(wg.at[core], wg.at[core], sems.at[22], sems.at[23], seq_of(z, y, 1 - core), x)
+    last.start()
+    last.wait()
+
+
+def incoming_kernel(cot_ref, w_ref, got_ref, wg_ref, slots, send, recv, sems):
+    greet(False)
+    exchange_start(cot_ref, got_ref, send, recv)
+    gather_out_weight(w_ref, slots, wg_ref, sems)
+    exchange_wait(cot_ref, got_ref, send, recv)
+
+
+def incoming(cot, w_out):
+    vmem = pl.BlockSpec(memory_space=pltpu.VMEM)
+    return pl.pallas_call(
+        incoming_kernel,
+        out_shape=(
+            jax.ShapeDtypeStruct((SEQ, GROUP, D), BF16),
+            jax.ShapeDtypeStruct((2, NZ, NY, 48, HALF), BF16),
+        ),
+        in_specs=[vmem, vmem],
+        out_specs=(vmem, vmem),
+        scratch_shapes=[
+            pltpu.VMEM((2, 32, D), BF16),
+            pltpu.SemaphoreType.DMA,
+            pltpu.SemaphoreType.DMA,
+            pltpu.SemaphoreType.DMA((24,)),
+        ],
+        compiler_params=pltpu.CompilerParams(
+            collective_id=0, has_side_effects=True, vmem_limit_bytes=LIMIT
+        ),
+    )(cot, w_out)
+
+
+def scatter_weight(at_ref, bg_ref, out, bufs, sems, norm_scale):
+    at2, bg2, wsum, wb, xr, s1, wb2, yr, zs, zr, s3 = bufs
+    seq, x, z, y, core = place()
+    other = 1 - core
+    partner = seq_of(z, y, other)
+    mine = pl.multiple_of(core * HALF, 128)
+    theirs = pl.multiple_of(other * HALF, 128)
+    c0 = remote(at_ref, at2, sems.at[0], sems.at[1], partner, x)
+    c1 = remote(bg_ref.at[:, pl.ds(theirs, HALF)], bg2, sems.at[2], sems.at[3], partner, x)
+    c0.start()
+    c1.start()
+    c0.wait()
+    c1.wait()
+
+    @pl.loop(0, NX)
+    def _(i):
+        for j in range(NY):
+            rows = pl.ds(pl.multiple_of((i * NY + j) * 80, 16), 80)
+            part = jnp.dot(at_ref[rows, :], bg_ref[:, pl.ds(mine, HALF)], preferred_element_type=F32)
+            part += jnp.dot(at2[rows, :], bg2[...], preferred_element_type=F32)
+            wsum[i, j] = part
+            wb[i, j] = part.astype(BF16)
+
+    copies = []
+    for k in range(1, NX):
+        to = lax.rem(x + k, NX)
+        copies.append(remote(wb.at[to], xr.at[k - 1], sems.at[2 + 2 * k], sems.at[3 + 2 * k], seq, to))
+    for one in copies:
+        one.start()
+    for one in copies:
+        one.wait()
+
+    for j in range(NY):
+        total = wsum[x, j]
+        for k in range(3):
+            total += xr[k, j].astype(F32)
+        s1[j] = total
+        wb2[j] = total.astype(BF16)
+    copies = []
+    for k in range(1, NY):
+        to = lax.rem(y + k, NY)
+        copies.append(
+            remote(wb2.at[to], yr.at[k - 1], sems.at[8 + 2 * k], sems.at[9 + 2 * k], seq_of(z, to, core), x)
+        )
+    for one in copies:
+        one.start()
+    for one in copies:
+        one.wait()
+    total = s1[y]
+    for k in range(3):
+        total += yr[k].astype(F32)
+    r, c = pick(128, 80, 0)
+    low = lax.rem(r, 16)
+    chosen = jnp.where((c == lax.div(r, 16) * 10 + low) & (low < 10), 1.0, 0.0).astype(BF16)
+    zs[...] = jnp.dot(chosen, total.astype(BF16), preferred_element_type=F32).astype(BF16)
+    copies = []
+    for k in range(1, NZ):
+        to = lax.rem(z + k, NZ)
+        src = zs.at[pl.ds(pl.multiple_of(to * 16, 16), 16)]
+        copies.append(remote(src, zr.at[k - 1], sems.at[14 + 2 * k], sems.at[15 + 2 * k], seq_of(to, y, core), x))
+    for one in copies:
+        one.start()
+    for one in copies:
+        one.wait()
+    total = zs[pl.ds(pl.multiple_of(z * 16, 16), 16), :].astype(F32)
+    for k in range(7):
+        total += zr[k].astype(F32)
+    s3[...] = total * norm_scale
+    owner = 16 * x + 4 * y + lax.div(z, 2)
+    slot = out.at[lax.rem(z, 2), core]
+
+    @pl.when(owner != seq)
+    def _():
+        one = remote(s3, slot, sems.at[30], sems.at[31], owner, x)
+        one.start()
+        one.wait_send()
+
+    @pl.when(owner == seq)
+    def _():
+        pltpu.make_async_copy(s3, slot, sems.at[31]).start()
+
+    holds = x == lax.div(seq, 16)
+
+    @pl.when(holds)
+    def _():
+        pltpu.make_async_copy(out, out, sems.at[31]).wait()
+        copies = []
+        for k in range(1, NX):
+            copies.append(remote(out, out, sems.at[31 + k], sems.at[35], seq, lax.rem(x + k, NX)))
+        for one in copies:
+            one.start()
+        for one in copies:
+            one.wait_send()
+
+    @pl.when(jnp.logical_not(holds))
+    def _():
+        pltpu.make_async_copy(out, out, sems.at[35]).wait()
+
+
+def sum_gain(gain_ref, out_ref, g1, g2, ghold, sems, norm_scale):
+    seq, x, z, y, core = place()
+    copies = []
+    for k in range(1, 16):
+        kx, ky = k // 4, k % 4
+        to = seq_of(z, lax.rem(y + ky, NY), core)
+        copies.append(
+            remote(gain_ref, g1.at[k - 1], sems.at[2 * k - 2], sems.at[2 * k - 1], to, lax.rem(x + kx, NX))
+        )
+    for one in copies:
+        one.start()
+    for one in copies:
+        one.wait()
+    total = gain_ref[...]
+    for k in range(15):
+        total += g1[k]
+    ghold[...] = total
+    copies = []
+    for k in range(1, 16):
+        kz, kc = k // 2, k % 2
+        to = seq_of(lax.rem(z + kz, NZ), y, lax.rem(core + kc, 2))
+        copies.append(remote(ghold, g2.at[k - 1], sems.at[28 + 2 * k], sems.at[29 + 2 * k], to, x))
+    for one in copies:
+        one.start()
+    for one in copies:
+        one.wait()
+    for k in range(15):
+        total += g2[k]
+    out_ref[...] = total * norm_scale
+
+
+def outgoing_kernel(
+    norm_scale, tok_ref, at_ref, bg_ref, gain_ref, got_ref, dw_ref, dg_ref,
+    at2, bg2, wsum, wb, xr, s1, wb2, yr, zs, zr, s3, g1, g2, ghold, send, recv, sems, gsems,
+):
+    greet(True)
+    exchange_start(tok_ref, got_ref, send, recv)
+    scatter_weight(
+        at_ref, bg_ref, dw_ref, (at2, bg2, wsum, wb, xr, s1, wb2, yr, zs, zr, s3), sems, norm_scale
+    )
+    sum_gain(gain_ref, dg_ref, g1, g2, ghold, gsems, norm_scale)
+    exchange_wait(tok_ref, got_ref, send, recv)
+
+
+def outgoing(tok, at, bg, gain_terms, norm_scale):
+    vmem = pl.BlockSpec(memory_space=pltpu.VMEM)
+
+    def kernel(*refs):
+        return outgoing_kernel(norm_scale, *refs)
+
+    return pl.pallas_call(
+        kernel,
+        out_shape=(
+            jax.ShapeDtypeStruct((SEQ, GROUP, D), BF16),
+            jax.ShapeDtypeStruct((2, 2, 16, HALF), F32),
+            jax.ShapeDtypeStruct((10, 128), F32),
+        ),
+        in_specs=[vmem] * 4,
+        out_specs=(vmem,) * 3,
+        scratch_shapes=[
+            pltpu.VMEM((D, 256), BF16),
+            pltpu.VMEM((256, HALF), BF16),
+            pltpu.VMEM((NX, NY, 80, HALF), F32),
+            pltpu.VMEM((NX, NY, 80, HALF), BF16),
+            pltpu.VMEM((3, NY, 80, HALF), BF16),
+            pltpu.VMEM((NY, 80, HALF), F32),
+            pltpu.VMEM((NY, 80, HALF), BF16),
+            pltpu.VMEM((3, 80, HALF), BF16),
+            pltpu.VMEM((128, HALF), BF16),
+            pltpu.VMEM((7, 16, HALF), BF16),
+            pltpu.VMEM((16, HALF), F32),
+            pltpu.VMEM((15, 10, 128), F32),
+            pltpu.VMEM((15, 10, 128), F32),
+            pltpu.VMEM((10, 128), F32),
+            pltpu.SemaphoreType.DMA,
+            pltpu.SemaphoreType.DMA,
+            pltpu.SemaphoreType.DMA((36,)),
+            pltpu.SemaphoreType.DMA((60,)),
+        ],
+        compiler_params=pltpu.CompilerParams(
+            collective_id=1, has_side_effects=True, vmem_limit_bytes=LIMIT
+        ),
+    )(tok, at, bg, gain_terms)
 
 
 def image_mask(shard_lengths, row_count):
@@ -58,9 +393,6 @@
     head_size = model_width // HEADS
     score_scale = 1.0 / math.sqrt(head_size)
     incoming = block_grad.astype(jnp.float32)
-    weight_grad = lax.dot_general(
-        attended, block_grad, (((0,), (0,)), ((), ())), preferred_element_type=jnp.float32
-    )
     grad_attended = lax.dot_general(
         block_grad, w_out, (((1,), (1,)), ((), ())), preferred_element_type=jnp.float32
     )
@@ -100,38 +432,34 @@
         - standard * jnp.mean(grad_standard * standard, axis=-1, keepdims=True)
     )
     patch_grad = (incoming + grad_branch).astype(jnp.bfloat16)
-    return (patch_grad, weight_grad, gain_grad)
+    return (patch_grad, gain_grad)
 
 
 def per_device(patches, lengths, token_dest, gain, w_qkv, w_out, cotangent):
-    full_out = lax.all_gather(w_out, "seq", axis=0, tiled=True)
+    returned, wg = incoming(cotangent[0].reshape(SEQ, GROUP, D), w_out)
+    full_out = jnp.transpose(wg[:, :, :, :40], (1, 2, 3, 0, 4)).reshape(D, D)
     patch_rows = patches[0]
     row_count, model_width = patch_rows.shape
     block, saved = forward(patch_rows, lengths[0, 0], gain, w_qkv, full_out)
-    seq_count = lax.axis_size("seq")
     token_count = row_count // GROUP
-    peer_count = token_count // seq_count
     tokens = block.reshape(token_count, GROUP * model_width)
-    targets = token_dest[0]
-    slot_ids = targets // token_count * peer_count + targets % peer_count
-    placing = (slot_ids[:, None] == jnp.arange(token_count, dtype=jnp.int32)[None, :]).astype(
-        jnp.bfloat16
-    )
-    outgoing = lax.dot_general(
+    slot_ids = token_dest[0] // token_count
+    placing = (slot_ids[:, None] == jnp.arange(token_count, dtype=jnp.int32)[None, :]).astype(BF16)
+    sent = lax.dot_general(
         placing, tokens, (((0,), (0,)), ((), ())), preferred_element_type=jnp.float32
-    ).astype(jnp.bfloat16)
-    merged = lax.all_to_all(outgoing, "seq", split_axis=0, concat_axis=0, tiled=True)
-    returned = lax.all_to_all(cotangent[0], "seq", split_axis=0, concat_axis=0, tiled=True)
-    token_grad = jnp.dot(placing, returned, preferred_element_type=jnp.float32).astype(jnp.bfloat16)
+    ).astype(BF16)
+    token_grad = jnp.dot(
+        placing, returned.reshape(SEQ, GROUP * D), preferred_element_type=jnp.float32
+    ).astype(BF16)
     block_grad = token_grad.reshape(row_count, model_width)
-    patch_grad, weight_grad, gain_grad = backward(saved, block_grad, gain, w_qkv, full_out)
-    share = model_width // seq_count
-    total_weight, total_gain = lax.psum((weight_grad, gain_grad), ("seq", "dp"))
-    first_row = lax.axis_index("seq") * share
-    own_weight = lax.dynamic_slice_in_dim(total_weight, first_row, share, 0)
-    own_gain = lax.dynamic_slice_in_dim(total_gain, first_row, share, 0)
-    norm_scale = 1.0 / math.sqrt(row_count * seq_count * lax.axis_size("dp"))
-    return (merged[None], patch_grad[None], own_weight * norm_scale, own_gain * norm_scale)
+    patch_grad, gain_grad = backward(saved, block_grad, gain, w_qkv, full_out)
+    norm_scale = 1.0 / math.sqrt(row_count * SEQ * NX)
+    merged, dw, dg = outgoing(
+        sent.reshape(SEQ, GROUP, D), saved[7].T, block_grad, gain_grad.reshape(10, 128), norm_scale
+    )
+    own_weight = jnp.transpose(dw[:, :, :10], (0, 2, 1, 3)).reshape(20, D)
+    own_gain = lax.dynamic_slice_in_dim(dg.reshape(D), lax.axis_index("seq") * 20, 20, 0)
+    return (merged.reshape(1, SEQ, GROUP * D), patch_grad[None], own_weight, own_gain)
 
 
 def solution(mesh):

time: 470 us -> 219 us (0.47)
  waiting for transfers between devices: 276 us -> 0 us
  Pallas kernels: 0 us -> 141 us
  blocking collectives: 76.7 us -> 0 us
  starting transfers between devices: 24.2 us -> 0 us
  between operations: 15.7 us -> 0.85 us
  local copies, waits for them, and re-layouts: 14.1 us -> 21.1 us
  matrix products: 54.7 us -> 50 us
    psum x1 -> x0, waiting for transfers between devices: 273 us -> none  [per_device(): total_weight, total_gain = lax.psum((weight_grad, gain_grad), ('seq', 'dp'))]
    pallas_call x0 -> x2, Pallas kernels: none -> 141 us  [the longest x1 72.5 us: outgoing(): pl.pallas_call(kernel, out_shape=(jax.ShapeDtypeStruct((SEQ, GROUP, D), B...]
    psum x1 -> x0, blocking collectives: 76.7 us -> none  [per_device(): total_weight, total_gain = lax.psum((weight_grad, gain_grad), ('seq', 'dp'))]
    all_to_all x2 -> x0, starting transfers between devices: 23.9 us -> none  [the longest x1 13.2 us: per_device(): lax.all_to_all(cotangent[0], 'seq', split_axis=0, concat_axis=0, tiled=True)]
    unnamed x28 -> x30, local copies, waits for them, and re-layouts: 10.9 us -> 4.04 us
    transpose x0 -> x4, local copies, waits for them, and re-layouts: none -> 5.66 us  [the longest x2 5.59 us: per_device(): full_out = jnp.transpose(wg[:, :, :, :40], (1, 2, 3, 0, 4)).reshape(D, D)]
    dot_general x2 -> x1, matrix products: 5.19 us -> 0.38 us  [per_device(): jnp.dot(placing, returned.reshape(SEQ, GROUP * D), preferred_element_type...]
  transfers between devices with their start and end apart: 4 -> 0, of which waited for: 2 -> 0; matrix products, arithmetic and copies ran while one was open for 6% -> 0% of each run, Pallas kernels for 0% -> 0%
where the time goes in v1:
time: 219 us; the launch traced here: 218 us
  Pallas kernels  141 us (64%)
  matrix products  50 us (23%)
  local copies, waits for them, and re-layouts  21.1 us (10%)
  other arithmetic  5.75 us (3%)
    pallas_call x1, Pallas kernels, outgoing(): pl.pallas_call(kernel, out_shape=(jax.ShapeDtypeStruct((SEQ, GROUP, D), B...  72.5 us
    pallas_call x1, Pallas kernels, incoming(): pl.pallas_call(incoming_kernel, out_shape=(jax.ShapeDtypeStruct((SEQ, GRO...  68.1 us
    dot_general x1, matrix products, backward(): jnp.einsum('hqk,khe->qhe', grad_scores, key_rows, preferred_element_type=...  8.36 us
    dot_general x1, matrix products, backward(): jnp.einsum('hqk,qhe->khe', grad_scores, queries, preferred_element_type=j...  8.11 us
    dot_general x1, matrix products, backward(): lax.dot_general(grad_projected, w_qkv, (((1,), (1,)), ((), ())), preferre...  7.89 us
    dot_general x1, matrix products, forward(): jnp.dot(normed, w_qkv, preferred_element_type=jnp.float32)  6.86 us
    transpose x2, local copies, waits for them, and re-layouts, per_device(): full_out = jnp.transpose(wg[:, :, :, :40], (1, 2, 3, 0, 4)).reshape(D, D)  5.59 us

profile of v1, /device:TPU:1, one launch (start us, length us, event | category | flops | bytes accessed | tf_op | source)
XLA Modules:
  0.0 218.4 jit_solution(26411952172854217)
XLA Ops:
  0.6 0.7 and_select_fusion
  1.3 0.7 multiply_bitcast_fusion
  2.0 0.2 reduce-window.8
  2.1 0.1 convert_reduce_fusion.1
  2.2 1.3 convert_reduce_fusion
  3.5 1.4 fusion.44
  4.9 0.1 broadcast_compare_fusion
  5.0 2.5 %reshape_squeeze.3.cot_ref = bf16[64,4,1280]{2,1,0:T(4,128)(2,1)} reshape(bf16[1,64,5120]{2,1,0:T(8,128)(2,1)} %param.13) | data formatting | bytes 1310720 | tf_op jit(solution)/shard_map/reshape;squeeze | solution.py:439
  7.6 6.9 %convolution_convert_fusion.2 = bf16[256,3840]{1,0:T(8,128)(2,1)S(1)} fusion(bf16[1280,3840]{1,0:T(8,128)(2,1)} %param.11, bf16[1,256,1280]{2,1,0:T(8,128)(2,1)} %param.7, f32[1280]{0:T(1024)} %param.10, f32[256]{0:T(256)S(1)} %add_rsqrt_fusion, f32[256]{0:T(256)S(1)} %broadcast_multiply_fusion.2), kind=kOutput, calls=%fused_computation.4 | convolution fusion | flops 2519203840 | bytes 12459008 | tf_op jit(solution)/shard_map/dot_general | solution.py:366
  14.4 0.1 fusion.63
  14.6 1.1 copy.35
  15.6 0.2 copy.34
  15.9 0.0 copy-start.6
  15.9 0.2 copy.33
  16.1 68.1 %shard_map.102 = (bf16[64,4,1280]{2,1,0:T(4,128)(2,1)}, bf16[2,8,4,48,640]{4,3,2,1,0:T(8,128)(2,1)}) custom-call(bf16[64,4,1280]{2,1,0:T(4,128)(2,1)} %reshape_squeeze.3.cot_ref, bf16[20,1280]{1,0:T(8,128)(2,1)} %w_ref.1), custom_call_target="tpu_custom_call" | custom-call | tf_op jit(solution)/shard_map/pallas_call | solution.py:146
  84.3 2.2 %slice_bitcast_fusion = bf16[8,4,40,2,640]{4,2,1,0,3:T(8,128)(2,1)S(1)} fusion(bf16[2,8,4,48,640]{4,3,2,1,0:T(8,128)(2,1)} %get-tuple-element.9), kind=kLoop, calls=%fused_computation.10 | loop fusion | bytes 6553600 | tf_op jit(solution)/shard_map/transpose | solution.py:440
  86.5 3.4 %copy.37 = bf16[8,4,40,2,640]{4,3,2,1,0:T(2,128)(2,1)S(1)} copy(bf16[8,4,40,2,640]{4,2,1,0,3:T(8,128)(2,1)S(1)} %slice_bitcast_fusion) | data formatting | bytes 6553600 | tf_op jit(solution)/shard_map/transpose | solution.py:440
  89.9 2.3 %copy.47 = bf16[160,8,2,640]{3,1,2,0:T(8,128)(2,1)} copy(bf16[160,8,2,640]{3,2,1,0:T(2,128)(2,1)S(1)} %bitcast.101) | data formatting | bytes 6553600
  92.2 0.0 copy-done.8
  92.2 0.1 copy.48
  92.3 0.4 convolution_convert_fusion
  92.7 0.4 reshape.180.refs_2_
  93.1 0.0 copy-start.4
  93.1 4.1 %convolution_convert_fusion.3 = bf16[256,1280]{1,0:T(8,128)(2,1)} fusion(bf16[256,1280]{1,0:T(8,128)(2,1)S(1)} %reshape.180.refs_2_, bf16[1280,1280]{1,0:T(8,128)(2,1)} %bitcast.102), kind=kOutput, calls=%fused_computation.14 | convolution fusion | flops 839188480 | bytes 4587520 | tf_op jit(solution)/shard_map/dot_general | solution.py:396
  97.2 1.3 copy.38
  98.5 0.0 copy-done.1
  98.5 0.0 copy-done.6
  98.5 0.0 copy-done.4
  98.5 3.4 %fusion.64 = (f32[16,256]{1,0:T(8,128)S(1)}, f32[16,256,256]{1,2,0:T(8,128)}) fusion(pred[256,256]{0,1:T(8,128)(4,1)S(1)} %broadcast_compare_fusion, bf16[256,16,80]{0,2,1:T(8,128)(2,1)S(1)} %bitcast.111, bf16[256,16,80]{0,2,1:T(8,128)(2,1)S(1)} %bitcast.109), kind=kOutput, calls=%fused_computation.83 | convolution fusion | flops 171966720 | bytes 5586944 | tf_op jit(solution)/shard_map/sub | solution.py:377
  101.9 2.8 %convolution_convert_fusion.5 = bf16[16,80,256]{2,1,0:T(8,128)(2,1)S(1)} fusion(bf16[256,16,80]{0,2,1:T(8,128)(2,1)S(1)} %bitcast.105, f32[16,256,256]{1,2,0:T(8,128)} %get-tuple-element.21, f32[16,256]{1,0:T(8,128)S(1)} %get-tuple-element.20), kind=kOutput, calls=%fused_computation.41 | convolution fusion | flops 170196992 | bytes 5521408 | tf_op jit(solution)/shard_map/hqk,khe->qhe/dot_general | solution.py:380
  104.8 0.9 copy-done.9
  105.7 1.1 fusion.6
  106.7 0.4 reshape.177
  107.1 0.5 convolution_convert_fusion.1
  107.6 1.3 reshape.178.refs_0_
  108.9 3.8 %convolution_convert_fusion.4 = bf16[16,80,256]{2,1,0:T(8,128)(2,1)} fusion(bf16[256,16,80]{0,2,1:T(8,128)(2,1)S(1)} %bitcast.107, f32[16,256,256]{1,2,0:T(8,128)} %get-tuple-element.21, f32[16,256]{1,0:T(8,128)S(1)} %get-tuple-element.20), kind=kOutput, calls=%fused_computation.40 | convolution fusion | flops 170196992 | bytes 5521408 | tf_op jit(solution)/shard_map/hqk,qhe->khe/dot_general | solution.py:403
  112.8 2.7 %fusion.65 = f32[16,256,256]{1,2,0:T(8,128)} fusion(bf16[256,16,80]{0,2,1:T(8,128)(2,1)S(1)} %bitcast.108, bf16[256,16,80]{0,2,1:T(8,128)(2,1)S(1)} %bitcast.106), kind=kOutput, calls=%fused_computation.84 | convolution fusion | flops 167772160 | bytes 5505024 | tf_op jit(solution)/shard_map/qhe,khe->hqk/dot_general | solution.py:400
  115.5 8.4 %fusion.31 = bf16[16,80,256]{2,1,0:T(8,128)(2,1)} fusion(bf16[256,16,80]{0,2,1:T(8,128)(2,1)S(1)} %bitcast.110, f32[16,256,256]{1,2,0:T(8,128)} %fusion.65, f32[16,256,256]{1,2,0:T(8,128)} %get-tuple-element.21, f32[16,256]{1,0:T(8,128)S(1)} %get-tuple-element.20), kind=kOutput, calls=%fused_computation.38 | convolution fusion | flops 175444224 | bytes 9715712 | tf_op jit(solution)/shard_map/hqk,khe->qhe/dot_general | solution.py:410
  123.8 0.0 copy-done.7
  123.8 8.1 %fusion.34 = bf16[16,80,256]{2,1,0:T(8,128)(2,1)} fusion(bf16[256,16,80]{0,2,1:T(8,128)(2,1)S(1)} %bitcast.112, f32[16,256,256]{1,2,0:T(8,128)} %fusion.65, f32[16,256,256]{1,2,0:T(8,128)} %get-tuple-element.21, f32[16,256]{1,0:T(8,128)S(1)} %get-tuple-element.20), kind=kOutput, calls=%fused_computation.39 | convolution fusion | flops 175444224 | bytes 9715712 | tf_op jit(solution)/shard_map/hqk,qhe->khe/dot_general | solution.py:413
  132.0 7.9 %fusion.39 = (f32[256]{0:T(256)S(1)}, f32[1280]{0:T(1024)}, f32[256]{0:T(256)S(1)}, f32[256,1280]{1,0:T(8,128)S(1)}) fusion(bf16[1,256,1280]{2,1,0:T(8,128)(2,1)S(1)} %copy-done, f32[1280]{0:T(1024)S(1)} %copy-done.11, f32[256]{0:T(256)S(1)} %add_rsqrt_fusion, f32[256]{0:T(256)S(1)} %broadcast_multiply_fusion.2, bf16[1280,3840]{1,0:T(8,128)(2,1)} %param.11, ...), kind=kOutput, calls=%fused_computation.44 | convolution fusion | flops 2525427968 | bytes 13776896 | tf_op jit(solution)/shard_map/dot_general | solution.py:424
  139.9 72.5 %shard_map.103 = (bf16[64,4,1280]{2,1,0:T(4,128)(2,1)}, f32[2,2,16,640]{3,2,1,0:T(8,128)}, f32[10,128]{1,0:T(8,128)}) custom-call(bf16[64,4,1280]{2,1,0:T(4,128)(2,1)} %reshape.178.refs_0_, bf16[1280,256]{1,0:T(8,128)(2,1)} %bitcast.115, bf16[256,1280]{1,0:T(8,128)(2,1)} %copy-done.1, f32[10,128]{1,0:T(8,128)} %bitcast.119), custom_call_target="tpu_custom_call" | custom-call | tf_op jit(solution)/shard_map/pallas_call | solution.py:315
  212.4 0.0 copy-start.10
  212.4 1.3 dynamic_slice.3
  213.7 2.4 %reshape.186 = bf16[1,64,5120]{2,1,0:T(8,128)(2,1)} reshape(bf16[64,4,1280]{2,1,0:T(4,128)(2,1)} %get-tuple-element.11) | data formatting | bytes 1310720 | tf_op jit(solution)/shard_map/reshape | solution.py:462
  216.2 1.4 fusion.47
  217.6 0.1 copy.42
  217.7 0.7 copy.49
  (22 shorter events, 0.1 us)
Async XLA Ops:
  15.9 82.6 %copy-start.6 = (bf16[256,1280]{0,1:T(8,128)(2,1)}, bf16[256,1280]{0,1:T(8,128)(2,1)S(1)}, u32[]{:S(2)}) copy-start(bf16[256,1280]{0,1:T(8,128)(2,1)S(1)} %copy.34) | copy-start | bytes 1966084
  89.9 2.4 %copy-start.8 = (bf16[64,4,1280]{2,1,0:T(4,128)(2,1)S(1)}, bf16[64,4,1280]{2,1,0:T(4,128)(2,1)}, u32[]{:S(2)}) copy-start(bf16[64,4,1280]{2,1,0:T(4,128)(2,1)} %get-tuple-element.10) | copy-start | bytes 1966084
  93.1 5.4 %copy-start.1 = (bf16[256,1280]{1,0:T(8,128)(2,1)}, bf16[256,1280]{1,0:T(8,128)(2,1)S(1)}, u32[]{:S(2)}) copy-start(bf16[256,1280]{1,0:T(8,128)(2,1)S(1)} %reshape.180.refs_2_) | copy-start | bytes 1966084
  93.1 5.4 %copy-start.4 = (bf16[256,1280]{0,1:T(8,128)(2,1)S(1)}, bf16[256,1280]{0,1:T(8,128)(2,1)}, u32[]{:S(2)}) copy-start(bf16[256,1280]{0,1:T(8,128)(2,1)} %copy.35) | copy-start | bytes 1966084
  101.9 3.7 %copy-start = (bf16[1,256,1280]{2,1,0:T(8,128)(2,1)S(1)}, bf16[1,256,1280]{2,1,0:T(8,128)(2,1)}, u32[]{:S(2)}) copy-start(bf16[1,256,1280]{2,1,0:T(8,128)(2,1)} %param.7) | copy-start | bytes 1966084
  101.9 3.7 %copy-start.3 = (bf16[160,8,2,640]{3,1,2,0:T(8,128)(2,1)S(1)}, bf16[160,8,2,640]{3,1,2,0:T(8,128)(2,1)}, u32[]{:S(2)}) copy-start(bf16[160,8,2,640]{3,1,2,0:T(8,128)(2,1)} %copy.47) | copy-start | bytes 9830404
  104.8 0.9 copy-start.9
  112.8 2.7 %copy-start.5 = (bf16[256,1280]{0,1:T(8,128)(2,1)S(1)}, bf16[256,1280]{0,1:T(8,128)(2,1)}, u32[]{:S(2)}) copy-start(bf16[256,1280]{0,1:T(8,128)(2,1)} %copy.35) | copy-start | bytes 1966084
  115.5 8.4 %copy-start.7 = (bf16[256,1280]{0,1:T(8,128)(2,1)S(1)}, bf16[256,1280]{0,1:T(8,128)(2,1)}, u32[]{:S(2)}) copy-start(bf16[256,1280]{0,1:T(8,128)(2,1)} %copy-done.6) | copy-start | bytes 1966084
  123.8 8.1 %copy-start.11 = (f32[1280]{0:T(1024)S(1)}, f32[1280]{0:T(1024)}, u32[]{:S(2)}) copy-start(f32[1280]{0:T(1024)} %param.10) | copy-start | bytes 15364
  123.8 8.1 %copy-start.12 = (bf16[16,80,256]{2,1,0:T(8,128)(2,1)S(1)}, bf16[16,80,256]{2,1,0:T(8,128)(2,1)}, u32[]{:S(2)}) copy-start(bf16[16,80,256]{2,1,0:T(8,128)(2,1)} %convolution_convert_fusion.4) | copy-start | bytes 1966084
  139.9 76.3 %copy-start.2 = (bf16[256,1280]{1,0:T(8,128)(2,1)S(1)}, bf16[256,1280]{1,0:T(8,128)(2,1)}, u32[]{:S(2)}) copy-start(bf16[256,1280]{1,0:T(8,128)(2,1)} %copy-done.1) | copy-start | bytes 1966084
  212.4 5.2 %copy-start.10 = (f32[2,2,16,640]{3,2,1,0:T(8,128)S(1)}, f32[2,2,16,640]{3,2,1,0:T(8,128)}, u32[]{:S(2)}) copy-start(f32[2,2,16,640]{3,2,1,0:T(8,128)} %get-tuple-element.12) | copy-start | bytes 491524

commit v2 on v0

v2 whole, which is shorter than its diff:
```python
import math

import jax
import jax.numpy as jnp
from jax import lax
from jax.experimental import pallas as pl
from jax.experimental.pallas import tpu as pltpu
from jax.sharding import PartitionSpec as P

HEADS = 16
GROUP = 4
D = 1280
HALF = 640
NZ, NY, NX = 8, 4, 4
SEQ = 64
LIMIT = 56 * 2**20

eps = 1e-06
F32 = jnp.float32
BF16 = jnp.bfloat16


def place():
    seq = lax.axis_index("seq")
    x = lax.axis_index("dp")
    return seq, x, lax.div(seq, 8), lax.rem(lax.div(seq, 2), 4), lax.rem(seq, 2)


def seq_of(z, y, core):
    return z * 8 + y * 2 + core


def dev(seq, x):
    return {"seq": seq, "dp": x}


def remote(src, dst, send, recv, seq, x):
    return pltpu.make_async_remote_copy(
        src_ref=src,
        dst_ref=dst,
        send_sem=send,
        recv_sem=recv,
        device_id=dev(seq, x),
        device_id_type=pl.DeviceIdType.MESH,
    )


def greet(with_xy):
    seq, x, z, y, core = place()
    barrier = pltpu.get_barrier_semaphore()

    @pl.loop(1, SEQ)
    def _(k):
        pl.semaphore_signal(
            barrier, inc=1, device_id=dev(lax.rem(seq + k, SEQ), x), device_id_type=pl.DeviceIdType.MESH
        )

    count = SEQ - 1
    if with_xy:
        for kx in range(1, NX):
            for ky in range(NY):
                pl.semaphore_signal(
                    barrier,
                    inc=1,
                    device_id=dev(seq_of(z, lax.rem(y + ky, NY), core), lax.rem(x + kx, NX)),
                    device_id_type=pl.DeviceIdType.MESH,
                )
                count += 1
    pl.semaphore_wait(barrier, count)


def exchange_start(src, dst, send, recv):
    seq, x, z, y, core = place()

    @pl.loop(1, SEQ)
    def _(k):
        to = lax.rem(seq + k, SEQ)
        remote(src.at[to], dst.at[seq], send, recv, to, x).start()

    pltpu.make_async_copy(src.at[seq], dst.at[seq], recv).start()


def exchange_wait(src, dst, send, recv):
    pltpu.make_async_copy(dst, dst, recv).wait()
    part = src.at[pl.ds(0, SEQ - 1)]
    pltpu.make_async_copy(part, part, send).wait()


def matmul(a, b):
    return jnp.dot(a, b, preferred_element_type=F32)


def matmul_t(a, b):
    return lax.dot_general(a, b, (((1,), (1,)), ((), ())), preferred_element_type=F32)


def one_hot(rows, columns, want):
    r = lax.broadcasted_iota(jnp.int32, (rows, columns), 0)
    c = lax.broadcasted_iota(jnp.int32, (rows, columns), 1)
    return jnp.where(want(r, c), 1.0, 0.0).astype(BF16)


WINDOWS = []
for _h in range(8):
    _first = 80 * _h // 128 * 128
    _off = 80 * _h - _first
    WINDOWS.append((_first, 128 if _off + 80 <= 128 else 256, _off))


def lanes_of(width, offset):
    lane = lax.broadcasted_iota(jnp.int32, (1, width), 1)
    return jnp.where((lane >= offset) & (lane < offset + 80), 1.0, 0.0).astype(BF16)


class Gather:
    def __init__(self, w_ref, slots, wg, sems):
        self.w_ref, self.slots, self.wg, self.sems = w_ref, slots, wg, sems

    def step0(self):
        seq, x, z, y, core = place()
        slots, sems = self.slots, self.sems
        own = jnp.concatenate([self.w_ref[...].astype(F32), jnp.zeros((12, D), F32)], axis=0)
        slots[core] = own.astype(BF16)
        self.now = [remote(slots.at[core], slots.at[core], sems.at[0], sems.at[1], seq_of(z, y, 1 - core), x)]
        self.start()

    def start(self):
        for one in self.now:
            one.start()

    def wait(self):
        for one in self.now:
            one.wait()

    def step1(self):
        seq, x, z, y, core = place()
        slots, sems, wg = self.slots, self.sems, self.wg
        self.wait()

        def want(r, c):
            return (c == jnp.where(r < 20, r, r + 12)) & (r < 40)

        first = pl.multiple_of(core * HALF, 128)
        rows = jnp.concatenate([slots[0, :, pl.ds(first, HALF)], slots[1, :, pl.ds(first, HALF)]], axis=0)
        wg[core, z, y] = matmul(one_hot(48, 64, want), rows).astype(BF16)
        self.now = []
        for k in range(1, NZ):
            self.now.append(
                remote(
                    wg.at[core, z, y], wg.at[core, z, y], sems.at[2 * k], sems.at[2 * k + 1],
                    seq_of(lax.rem(z + k, NZ), y, core), x,
                )
            )
        self.start()

    def step2(self):
        seq, x, z, y, core = place()
        sems, wg = self.sems, self.wg
        self.wait()
        self.now = []
        for k in range(1, NY):
            self.now.append(
                remote(
                    wg.at[core, :, y], wg.at[core, :, y], sems.at[14 + 2 * k], sems.at[15 + 2 * k],
                    seq_of(z, lax.rem(y + k, NY), core), x,
                )
            )
        self.start()

    def step3(self):
        seq, x, z, y, core = place()
        sems, wg = self.sems, self.wg
        self.wait()
        self.now = [remote(wg.at[core], wg.at[core], sems.at[22], sems.at[23], seq_of(z, y, 1 - core), x)]
        self.start()


class Scatter:
    def __init__(self, at_ref, bg_ref, out, bufs, sems, norm_scale):
        self.at_ref, self.bg_ref, self.out, self.bufs, self.sems = at_ref, bg_ref, out, bufs, sems
        self.norm_scale = norm_scale

    def start(self):
        for one in self.now:
            one.start()

    def wait(self):
        for one in self.now:
            one.wait()

    def send_attended(self):
        seq, x, z, y, core = place()
        partner = seq_of(z, y, 1 - core)
        self.now = [remote(self.at_ref, self.bufs[0], self.sems.at[0], self.sems.at[1], partner, x)]
        self.now[0].start()

    def send_grad(self):
        seq, x, z, y, core = place()
        partner = seq_of(z, y, 1 - core)
        theirs = pl.multiple_of((1 - core) * HALF, 128)
        one = remote(
            self.bg_ref.at[:, pl.ds(theirs, HALF)], self.bufs[1], self.sems.at[2], self.sems.at[3], partner, x
        )
        one.start()
        self.now.append(one)

    def product(self):
        at2, bg2, wsum, wb, xr, s1, wb2, yr, zs, zr, s3 = self.bufs
        seq, x, z, y, core = place()
        at_ref, bg_ref, sems = self.at_ref, self.bg_ref, self.sems
        mine = pl.multiple_of(core * HALF, 128)
        self.wait()

        @pl.loop(0, NX)
        def _(i):
            rows = pl.ds(pl.multiple_of(i * 320, 64), 320)
            part = matmul(at_ref[rows, :], bg_ref[:, pl.ds(mine, HALF)])
            part += matmul(at2[rows, :], bg2[...])
            part = part.reshape(NY, 80, HALF)
            wsum[i] = part
            wb[i] = part.astype(BF16)

        self.now = []
        for k in range(1, NX):
            to = lax.rem(x + k, NX)
            self.now.append(remote(wb.at[to], xr.at[k - 1], sems.at[2 + 2 * k], sems.at[3 + 2 * k], seq, to))
        self.start()

    def after_x(self):
        at2, bg2, wsum, wb, xr, s1, wb2, yr, zs, zr, s3 = self.bufs
        seq, x, z, y, core = place()
        sems = self.sems
        self.wait()

        @pl.loop(0, NY)
        def _(j):
            total = wsum[x, j]
            for k in range(3):
                total += xr[k, j].astype(F32)
            s1[j] = total
            wb2[j] = total.astype(BF16)

        self.now = []
        for k in range(1, NY):
            to = lax.rem(y + k, NY)
            self.now.append(
                remote(wb2.at[to], yr.at[k - 1], sems.at[8 + 2 * k], sems.at[9 + 2 * k], seq_of(z, to, core), x)
            )
        self.start()

    def after_y(self):
        at2, bg2, wsum, wb, xr, s1, wb2, yr, zs, zr, s3 = self.bufs
        seq, x, z, y, core = place()
        sems = self.sems
        self.wait()
        total = s1[y]
        for k in range(3):
            total += yr[k].astype(F32)

        def want(r, c):
            low = lax.rem(r, 16)
            return (c == lax.div(r, 16) * 10 + low) & (low < 10)

        zs[...] = matmul(one_hot(128, 80, want), total.astype(BF16)).astype(BF16)
        self.now = []
        for k in range(1, NZ):
            to = lax.rem(z + k, NZ)
            src = zs.at[pl.ds(pl.multiple_of(to * 16, 16), 16)]
            self.now.append(
                remote(src, zr.at[k - 1], sems.at[14 + 2 * k], sems.at[15 + 2 * k], seq_of(to, y, core), x)
            )
        self.start()

    def after_z(self):
        at2, bg2, wsum, wb, xr, s1, wb2, yr, zs, zr, s3 = self.bufs
        seq, x, z, y, core = place()
        sems, out = self.sems, self.out
        self.wait()
        total = zs[pl.ds(pl.multiple_of(z * 16, 16), 16), :].astype(F32)
        for k in range(7):
            total += zr[k].astype(F32)
        s3[...] = total * self.norm_scale
        owner = 16 * x + 4 * y + lax.div(z, 2)
        slot = out.at[lax.rem(z, 2), core]

        @pl.when(owner != seq)
        def _():
            remote(s3, slot, sems.at[30], sems.at[31], owner, x).start()

        @pl.when(owner == seq)
        def _():
            pltpu.make_async_copy(s3, slot, sems.at[31]).start()

    def share(self):
        seq, x, z, y, core = place()
        sems, out, s3 = self.sems, self.out, self.bufs[-1]
        owner = 16 * x + 4 * y + lax.div(z, 2)

        @pl.when(owner != seq)
        def _():
            pltpu.make_async_copy(s3, s3, sems.at[30]).wait()

        @pl.when(x == lax.div(seq, 16))
        def _():
            pltpu.make_async_copy(out, out, sems.at[31]).wait()
            for k in range(1, NX):
                remote(out, out, sems.at[31 + k], sems.at[35], seq, lax.rem(x + k, NX)).start()

    def finish(self):
        seq, x, z, y, core = place()
        sems, out = self.sems, self.out

        @pl.when(x == lax.div(seq, 16))
        def _():
            for k in range(1, NX):
                pltpu.make_async_copy(out, out, sems.at[31 + k]).wait()

        @pl.when(x != lax.div(seq, 16))
        def _():
            pltpu.make_async_copy(out, out, sems.at[35]).wait()


class GainSum:
    def __init__(self, ghold, g1, g2, sems):
        self.ghold, self.g1, self.g2, self.sems = ghold, g1, g2, sems

    def first(self, total):
        seq, x, z, y, core = place()
        self.ghold[0] = total
        self.now = []
        for k in range(1, 16):
            kx, ky = k // 4, k % 4
            to = seq_of(z, lax.rem(y + ky, NY), core)
            self.now.append(
                remote(
                    self.ghold.at[0], self.g1.at[k - 1], self.sems.at[2 * k - 2], self.sems.at[2 * k - 1],
                    to, lax.rem(x + kx, NX),
                )
            )
        for one in self.now:
            one.start()

    def second(self):
        seq, x, z, y, core = place()
        for one in self.now:
            one.wait()
        total = self.ghold[0]
        for k in range(15):
            total += self.g1[k]
        self.ghold[1] = total
        self.now = []
        for k in range(1, 16):
            kz, kc = k // 2, k % 2
            to = seq_of(lax.rem(z + kz, NZ), y, lax.rem(core + kc, 2))
            self.now.append(
                remote(
                    self.ghold.at[1], self.g2.at[k - 1], self.sems.at[28 + 2 * k], self.sems.at[29 + 2 * k], to, x
                )
            )
        for one in self.now:
            one.start()

    def finish(self):
        for one in self.now:
            one.wait()
        total = self.ghold[1]
        for k in range(15):
            total += self.g2[k]
        return total


def kernel_body(norm_scale, refs):
    (x_ref, rowi_ref, coli_ref, gain_ref, gaincol_ref, wqkv_hbm, wout_ref, cot_ref,
     merged_ref, gx_ref, dw_ref, dg_ref,
     wqkv, slots, wg, cslab, crecv, tok, got, xp, normed, kv, projt, eye, perm, permt, probs, at, atp, apad, bg, dat, gt, gn,
     at2, bg2, wsum, wb, xr, s1, wb2, yr, zs, zr, s3, ghold, g1, g2,
     wsem, asem, csend, crecvs, tsend, trecvs, ssem, gsem) = refs
    score_scale = 1.0 / math.sqrt(80)

    loads = []
    for j in range(3):
        cols = pl.ds(j * D, D)
        loads.append(pltpu.make_async_copy(wqkv_hbm.at[:, cols], wqkv.at[:, cols], wsem.at[j]))
    for one in loads:
        one.start()

    def shuffle(r, c):
        return c == lax.rem(r, 4) * 64 + lax.div(r, 4)

    stacked = jnp.concatenate([cot_ref[:, pl.ds(c * D, D)] for c in range(4)], axis=0)
    cslab[...] = matmul(one_hot(256, 256, shuffle), stacked).astype(BF16).reshape(SEQ, GROUP, D)
    greet(True)
    gather = Gather(wout_ref, slots, wg, asem)
    gather.step0()
    exchange_start(cslab, crecv, csend, crecvs)

    key_row, key_col = rowi_ref[0:1, :], coli_ref[:, 0:1]
    id_row, id_col = rowi_ref[1:2, :], coli_ref[:, 1:2]
    ir = lax.broadcasted_iota(jnp.int32, (256, 256), 0)
    ic = lax.broadcasted_iota(jnp.int32, (256, 256), 1)
    eye[...] = jnp.where(ir == ic, 1.0, 0.0).astype(BF16)
    perm[...] = jnp.where(ir == key_row, 1.0, 0.0).astype(BF16)
    permt[...] = jnp.where(ic == key_col, 1.0, 0.0).astype(BF16)
    ids_k = jnp.sum(jnp.where(ir == key_row, id_row.astype(F32), 0.0), axis=1, keepdims=True)
    ids_q = jnp.sum(jnp.where(ic == key_col, id_col.astype(F32), 0.0), axis=0, keepdims=True)

    wide = matmul(perm[...], x_ref[...])
    xp[...] = wide.astype(BF16)
    centred = wide - jnp.mean(wide, axis=-1, keepdims=True)
    spread = lax.rsqrt(jnp.mean(centred * centred, axis=-1, keepdims=True) + eps)
    normed[...] = (centred * spread * gain_ref[...]).astype(BF16)
    gather.step1()

    for j in range(3):
        loads[j].wait()

        @pl.loop(0, 5)
        def _(i):
            cols = pl.ds(pl.multiple_of(j * D + i * 256, 256), 256)
            part = matmul(normed[...], wqkv[:, cols]).astype(BF16)
            if j > 0:
                kv[:, pl.ds(pl.multiple_of((j - 1) * D + i * 256, 256), 256)] = part
            projt[cols, :] = matmul_t(eye[...], part).astype(BF16)

    gather.step2()
    same = ids_k == ids_q

    @pl.loop(0, 2)
    def _(g):
        for h in range(8):
            first, width, off = WINDOWS[h]
            lanes = pl.ds(pl.multiple_of(g * HALF + first, 128), width)
            rows = pl.multiple_of(g * HALF + h * 80, 16)
            keys = kv[:, lanes] * lanes_of(width, off)
            scores = matmul(keys, projt[lanes, :]) * score_scale
            scores = jnp.where(same, scores, -jnp.inf)
            scores = jnp.exp(scores - jnp.max(scores, axis=0, keepdims=True))
            share = scores * (1.0 / jnp.sum(scores, axis=0, keepdims=True))
            probs[g * 8 + h] = share
            part = matmul(projt[pl.ds(2 * D + rows, 80), :], share.astype(BF16))
            at[pl.ds(rows, 80), :] = part.astype(BF16)
            gap = jnp.zeros((8, 256), F32)
            padded = jnp.concatenate([part[0:40], gap, part[40:80], gap], axis=0).astype(BF16)
            atp[pl.ds(pl.multiple_of(g * 768 + h * 96, 16), 96), :] = padded

    gather.step3()
    scatter = Scatter(
        at, bg, dw_ref, (at2, bg2, wsum, wb, xr, s1, wb2, yr, zs, zr, s3), ssem, norm_scale
    )
    scatter.send_attended()
    exchange_wait(cslab, crecv, csend, crecvs)
    bg[...] = crecv[...].reshape(256, D)
    scatter.send_grad()
    for j in range(6):
        apad[:, pl.ds(j * 256, 256)] = matmul_t(eye[...], atp[pl.ds(j * 256, 256), :]).astype(BF16)
    scatter.product()

    gather.wait()
    for half in range(2):
        cols = pl.ds(half * HALF, HALF)
        branch = matmul(apad[...], wg[half].reshape(1536, HALF))
        block = (xp[:, cols].astype(F32) + branch).astype(BF16)
        tok[:, :, cols] = block.reshape(SEQ, GROUP, HALF)
    exchange_start(tok, got, tsend, trecvs)

    @pl.loop(0, 4)
    def _(i):
        part = matmul_t(wg[0, pl.ds(2 * i, 2)].reshape(384, HALF), bg[:, pl.ds(0, HALF)])
        part += matmul_t(wg[1, pl.ds(2 * i, 2)].reshape(384, HALF), bg[:, pl.ds(HALF, HALF)])
        for h in range(4):
            own = part[96 * h : 96 * h + 96]
            own = jnp.concatenate([own[0:40], own[48:88]], axis=0).astype(BF16)
            dat[pl.ds(pl.multiple_of(i * 320 + 80 * h, 16), 80), :] = own

    def back(g):
        for h in range(8):
            first, width, off = WINDOWS[h]
            lanes = pl.ds(pl.multiple_of(g * HALF + first, 128), width)
            rows = pl.multiple_of(g * HALF + h * 80, 16)
            values = kv[:, pl.ds(pl.multiple_of(D + g * HALF + first, 128), width)] * lanes_of(width, off)
            share = probs[g * 8 + h]
            gp = matmul(values, dat[lanes, :])
            delta = jnp.sum(gp * share, axis=0, keepdims=True)
            gs = (share * (gp - delta) * score_scale).astype(BF16)
            low = share.astype(BF16)
            gt[pl.ds(rows, 80), :] = matmul(projt[pl.ds(D + rows, 80), :], gs).astype(BF16)
            gt[pl.ds(D + rows, 80), :] = matmul_t(projt[pl.ds(rows, 80), :], gs).astype(BF16)
            gt[pl.ds(2 * D + rows, 80), :] = matmul_t(dat[pl.ds(rows, 80), :], low).astype(BF16)

    @pl.loop(0, 2)
    def _(g):
        back(g)

    scatter.after_x()

    def standard_of(i):
        return matmul_t(eye[...], xp[:, pl.ds(pl.multiple_of(i * 256, 256), 256)])

    def sums(i, carry):
        return carry + jnp.sum(standard_of(i), axis=0, keepdims=True)

    mean = lax.fori_loop(0, 5, sums, jnp.zeros((1, 256), F32)) * (1.0 / D)

    def squares(i, carry):
        part = standard_of(i) - mean
        return carry + jnp.sum(part * part, axis=0, keepdims=True)

    inv = lax.rsqrt(lax.fori_loop(0, 5, squares, jnp.zeros((1, 256), F32)) * (1.0 / D) + eps)

    def grads(i, carry):
        rows = pl.ds(pl.multiple_of(i * 256, 256), 256)
        part = matmul(wqkv[rows, :], gt[...])
        std = (standard_of(i) - mean) * inv
        both = part * std
        hi = both.astype(BF16)
        rest = both - hi.astype(F32)
        mid = rest.astype(BF16)
        lo = (rest - mid.astype(F32)).astype(BF16)
        ones = jnp.ones((8, 256), BF16)
        row = matmul_t(ones, hi) + matmul_t(ones, mid) + matmul_t(ones, lo)
        ghold[2, :, rows] = row[0:1]
        scaled = part * gaincol_ref[rows, :]
        gn[rows, :] = scaled
        a, b = carry
        return (a + jnp.sum(scaled, axis=0, keepdims=True), b + jnp.sum(scaled * std, axis=0, keepdims=True))

    zero = jnp.zeros((1, 256), F32)
    mean_g, mean_gs = lax.fori_loop(0, 5, grads, (zero, zero))
    gains = GainSum(ghold, g1, g2, gsem)
    gains.first(ghold[2])
    scatter.after_y()
    mean_g = mean_g * (1.0 / D)
    mean_gs = mean_gs * (1.0 / D)

    @pl.loop(0, 5)
    def _(i):
        rows = pl.ds(pl.multiple_of(i * 256, 256), 256)
        std = (standard_of(i) - mean) * inv
        branch = inv * (gn[rows, :] - mean_g - std * mean_gs)
        total = (matmul_t(eye[...], bg[:, rows]) + branch).astype(BF16)
        gx_ref[:, rows] = matmul_t(permt[...], total).astype(BF16)

    gains.second()
    scatter.after_z()
    exchange_wait(tok, got, tsend, trecvs)

    def unshuffle(r, c):
        return r == lax.rem(c, 4) * 64 + lax.div(c, 4)

    unmix = one_hot(256, 256, unshuffle)
    ordered = matmul(unmix, got[...].reshape(256, D)).astype(BF16)
    for c in range(4):
        merged_ref[:, pl.ds(c * D, D)] = ordered[64 * c : 64 * c + 64]
    scatter.share()
    dg_ref[...] = gains.finish() * norm_scale
    scatter.finish()


def per_device(patches, lengths, token_dest, gain, w_qkv, w_out, cotangent):
    norm_scale = 1.0 / math.sqrt(256 * SEQ * NX)
    row = jnp.arange(256, dtype=jnp.int32)
    slot = jnp.repeat(token_dest[0] // 64, GROUP)
    key = slot * GROUP + row % GROUP
    ends = jnp.cumsum(lengths[0, 0] * GROUP)
    ids = jnp.sum((row[:, None] >= ends[None, :]).astype(jnp.int32), axis=1)
    rows = jnp.stack([key, ids])
    columns = jnp.stack([key, ids], axis=1)
    vmem = pl.BlockSpec(memory_space=pltpu.VMEM)
    hbm = pl.BlockSpec(memory_space=pl.ANY)

    def kernel(*refs):
        kernel_body(norm_scale, refs)

    merged, gx, dw, dg = pl.pallas_call(
        kernel,
        out_shape=(
            jax.ShapeDtypeStruct((SEQ, GROUP * D), BF16),
            jax.ShapeDtypeStruct((256, D), BF16),
            jax.ShapeDtypeStruct((2, 2, 16, HALF), F32),
            jax.ShapeDtypeStruct((1, D), F32),
        ),
        in_specs=[vmem] * 5 + [hbm] + [vmem] * 2,
        out_specs=(vmem,) * 4,
        scratch_shapes=[
            pltpu.VMEM((D, 3 * D), BF16),
            pltpu.VMEM((2, 32, D), BF16),
            pltpu.VMEM((2, NZ, NY, 48, HALF), BF16),
            pltpu.VMEM((SEQ, GROUP, D), BF16),
            pltpu.VMEM((SEQ, GROUP, D), BF16),
            pltpu.VMEM((SEQ, GROUP, D), BF16),
            pltpu.VMEM((SEQ, GROUP, D), BF16),
            pltpu.VMEM((256, D), BF16),
            pltpu.VMEM((256, D), BF16),
            pltpu.VMEM((256, 2 * D), BF16),
            pltpu.VMEM((3 * D, 256), BF16),
            pltpu.VMEM((256, 256), BF16),
            pltpu.VMEM((256, 256), BF16),
            pltpu.VMEM((256, 256), BF16),
            pltpu.VMEM((HEADS, 256, 256), F32),
            pltpu.VMEM((D, 256), BF16),
            pltpu.VMEM((1536, 256), BF16),
            pltpu.VMEM((256, 1536), BF16),
            pltpu.VMEM((256, D), BF16),
            pltpu.VMEM((D, 256), BF16),
            pltpu.VMEM((3 * D, 256), BF16),
            pltpu.VMEM((D, 256), F32),
            pltpu.VMEM((D, 256), BF16),
            pltpu.VMEM((256, HALF), BF16),
            pltpu.VMEM((NX, NY, 80, HALF), F32),
            pltpu.VMEM((NX, NY, 80, HALF), BF16),
            pltpu.VMEM((3, NY, 80, HALF), BF16),
            pltpu.VMEM((NY, 80, HALF), F32),
            pltpu.VMEM((NY, 80, HALF), BF16),
            pltpu.VMEM((3, 80, HALF), BF16),
            pltpu.VMEM((128, HALF), BF16),
            pltpu.VMEM((7, 16, HALF), BF16),
            pltpu.VMEM((16, HALF), F32),
            pltpu.VMEM((3, 1, D), F32),
            pltpu.VMEM((15, 1, D), F32),
            pltpu.VMEM((15, 1, D), F32),
            pltpu.SemaphoreType.DMA((3,)),
            pltpu.SemaphoreType.DMA((24,)),
            pltpu.SemaphoreType.DMA,
            pltpu.SemaphoreType.DMA,
            pltpu.SemaphoreType.DMA,
            pltpu.SemaphoreType.DMA,
            pltpu.SemaphoreType.DMA((36,)),
            pltpu.SemaphoreType.DMA((60,)),
        ],
        compiler_params=pltpu.CompilerParams(
            collective_id=0, has_side_effects=True, vmem_limit_bytes=LIMIT
        ),
    )(
        patches[0], rows, columns, gain.reshape(1, D), gain.reshape(D, 1), w_qkv, w_out,
        cotangent[0],
    )
    own_weight = jnp.transpose(dw[:, :, :10], (0, 2, 1, 3)).reshape(20, D)
    own_gain = lax.dynamic_slice_in_dim(dg.reshape(D), lax.axis_index("seq") * 20, 20, 0)
    return (merged[None], gx[None], own_weight, own_gain)


def solution(mesh):
    placed = (
        P("dp", "seq", None),
        P("dp", "seq", None),
        P("dp", "seq"),
        P(),
        P(),
        P("seq", None),
        P("dp", "seq", None),
    )
    return jax.shard_map(
        per_device,
        mesh=mesh,
        in_specs=placed,
        out_specs=(P("dp", "seq", None), P("dp", "seq", None), P("seq", None), P("seq")),
        check_vma=False,
    )
```

time: 470 us -> 136 us (0.29)
  waiting for transfers between devices: 276 us -> 0 us
  Pallas kernels: 0 us -> 120 us
  blocking collectives: 76.7 us -> 0 us
  matrix products: 54.7 us -> 0 us
  starting transfers between devices: 24.2 us -> 0 us
  between operations: 15.7 us -> 0.68 us
  other arithmetic: 7.71 us -> 2.2 us
    psum x1 -> x0, waiting for transfers between devices: 273 us -> none  [per_device(): total_weight, total_gain = lax.psum((weight_grad, gain_grad), ('seq', 'dp'))]
    pallas_call x0 -> x1, Pallas kernels: none -> 120 us  [per_device(): pl.pallas_call(kernel, out_shape=(jax.ShapeDtypeStruct((SEQ, GROUP * D),...]
    psum x1 -> x0, blocking collectives: 76.7 us -> none  [per_device(): total_weight, total_gain = lax.psum((weight_grad, gain_grad), ('seq', 'dp'))]
    dot_general x12 -> x0, matrix products: 50.2 us -> none  [the longest x1 8.15 us: backward(): jnp.einsum('hqk,khe->qhe', grad_scores, key_rows, preferred_element_type=...]
    all_to_all x2 -> x0, starting transfers between devices: 23.9 us -> none  [the longest x1 13.2 us: per_device(): lax.all_to_all(cotangent[0], 'seq', split_axis=0, concat_axis=0, tiled=True)]
    unnamed x28 -> x4, local copies, waits for them, and re-layouts: 10.9 us -> 4.63 us
  transfers between devices with their start and end apart: 4 -> 0, of which waited for: 2 -> 0; matrix products, arithmetic and copies ran while one was open for 6% -> 0% of each run, Pallas kernels for 0% -> 0%
where the time goes in v2:
time: 136 us; the launch traced here: 134 us
  Pallas kernels  120 us (88%)
  local copies, waits for them, and re-layouts  11 us (8%)
  other arithmetic  2.2 us (2%)
    pallas_call x1, Pallas kernels, per_device(): pl.pallas_call(kernel, out_shape=(jax.ShapeDtypeStruct((SEQ, GROUP * D),...  120 us
    unnamed x4, local copies, waits for them, and re-layouts  4.63 us

profile of v2, /device:TPU:1, one launch (start us, length us, event | category | flops | bytes accessed | tf_op | source)
XLA Modules:
  0.0 133.9 jit_solution(2176100292216701085)
XLA Ops:
  0.6 0.7 fusion.2
  1.3 0.1 broadcast_in_dim.11
  1.4 0.1 mul.56
  1.5 0.7 multiply_bitcast_fusion
  2.2 0.2 reduce-window.8
  2.3 0.1 convert_reduce_fusion
  2.4 0.8 copy.18.refs_2_
  3.2 0.1 mul.52
  3.4 0.6 pad_add_fusion.refs_1_
  3.9 1.8 %reshape.130.refs_4_ = f32[1280,1]{1,0:T(8,128)} reshape(f32[1280]{0:T(1024)} %param.10) | data formatting | bytes 10240 | tf_op jit(solution)/shard_map/reshape | solution.py:634
  5.7 1.3 reshape.127.refs_3_
  7.0 120.0 %shard_map.102 = (bf16[64,5120]{1,0:T(8,128)(2,1)}, bf16[256,1280]{1,0:T(8,128)(2,1)}, f32[2,2,16,640]{3,2,1,0:T(8,128)}, f32[1,1280]{1,0:T(1,128)}) custom-call(bf16[256,1280]{1,0:T(8,128)(2,1)} %bitcast.29, s32[2,256]{1,0:T(2,128)} %pad_add_fusion.refs_1_, s32[256,2]{1,0:T(8,128)} %copy.18.refs_2_, f32[1,1280]{1,0:T(1,128)} %reshape.127.refs_3_, ...), custom_call_target="tpu_custom_call" | custom-call | tf_op jit(solution)/shard_map/pallas_call | solution.py:574
  127.0 1.3 dynamic-slice_bitcast_fusion
  128.3 0.9 slice_bitcast_fusion
  129.2 0.1 copy.20
  129.3 0.7 copy.21
  130.0 2.0 %copy.24 = bf16[1,64,5120]{2,1,0:T(8,128)(2,1)} copy(bf16[1,64,5120]{2,1,0:T(8,128)(2,1)} %bitcast.28) | data formatting | bytes 1310720
  132.0 2.0 %copy.25 = bf16[1,256,1280]{2,1,0:T(8,128)(2,1)} copy(bf16[1,256,1280]{2,1,0:T(8,128)(2,1)} %bitcast.27) | data formatting | bytes 1310720
  (4 shorter events, 0.1 us)

commit v3 on v2

--- a/solution.py
+++ b/solution.py
@@ -45,28 +45,38 @@
     )
 
 
-def greet(with_xy):
+def owner_of(x, y, z):
+    return 16 * x + 4 * y + lax.div(z, 2)
+
+
+def greet():
     seq, x, z, y, core = place()
     barrier = pltpu.get_barrier_semaphore()
 
+    def signal(to, where):
+        pl.semaphore_signal(barrier, inc=1, device_id=dev(to, where), device_id_type=pl.DeviceIdType.MESH)
+
     @pl.loop(1, SEQ)
     def _(k):
-        pl.semaphore_signal(
-            barrier, inc=1, device_id=dev(lax.rem(seq + k, SEQ), x), device_id_type=pl.DeviceIdType.MESH
-        )
-
-    count = SEQ - 1
-    if with_xy:
-        for kx in range(1, NX):
-            for ky in range(NY):
-                pl.semaphore_signal(
-                    barrier,
-                    inc=1,
-                    device_id=dev(seq_of(z, lax.rem(y + ky, NY), core), lax.rem(x + kx, NX)),
-                    device_id_type=pl.DeviceIdType.MESH,
-                )
-                count += 1
-    pl.semaphore_wait(barrier, count)
+        signal(lax.rem(seq + k, SEQ), x)
+
+    for kx in range(1, NX):
+        for ky in range(NY):
+            signal(seq_of(z, lax.rem(y + ky, NY), core), lax.rem(x + kx, NX))
+        signal(owner_of(x, y, z), lax.rem(x + kx, NX))
+
+    @pl.when(x != lax.div(seq, 16))
+    def _():
+        for part in range(2):
+            for other in range(2):
+                to = seq_of(2 * lax.rem(seq, 4) + part, lax.rem(lax.div(seq, 4), 4), other)
+                signal(to, lax.div(seq, 16))
+
+
+def all_here():
+    seq, x, z, y, core = place()
+    count = SEQ - 1 + 12 + 3 + jnp.where(x != lax.div(seq, 16), 4, 0)
+    pl.semaphore_wait(pltpu.get_barrier_semaphore(), count)
 
 
 def exchange_start(src, dst, send, recv):
@@ -115,70 +125,124 @@
 class Gather:
     def __init__(self, w_ref, slots, wg, sems):
         self.w_ref, self.slots, self.wg, self.sems = w_ref, slots, wg, sems
-
-    def step0(self):
+        self.p, self.q = pl.ds(0, 256), pl.ds(256, 384)
+
+    def pair(self):
         seq, x, z, y, core = place()
         slots, sems = self.slots, self.sems
         own = jnp.concatenate([self.w_ref[...].astype(F32), jnp.zeros((12, D), F32)], axis=0)
         slots[core] = own.astype(BF16)
-        self.now = [remote(slots.at[core], slots.at[core], sems.at[0], sems.at[1], seq_of(z, y, 1 - core), x)]
-        self.start()
-
-    def start(self):
-        for one in self.now:
-            one.start()
-
-    def wait(self):
-        for one in self.now:
-            one.wait()
-
-    def step1(self):
+        self.first = remote(slots.at[core], slots.at[core], sems.at[0], sems.at[1], seq_of(z, y, 1 - core), x)
+        self.first.start()
+
+    def along_z(self):
         seq, x, z, y, core = place()
         slots, sems, wg = self.slots, self.sems, self.wg
-        self.wait()
+        zh, zl = lax.div(z, 4), lax.rem(z, 4)
+        self.first.wait()
 
         def want(r, c):
             return (c == jnp.where(r < 20, r, r + 12)) & (r < 40)
 
         first = pl.multiple_of(core * HALF, 128)
         rows = jnp.concatenate([slots[0, :, pl.ds(first, HALF)], slots[1, :, pl.ds(first, HALF)]], axis=0)
-        wg[core, z, y] = matmul(one_hot(48, 64, want), rows).astype(BF16)
-        self.now = []
+        own = matmul(one_hot(48, 64, want), rows).astype(BF16)
+        wg[core, zh, zl, y, :, self.p] = own[:, 0:256]
+
+        @pl.when(zl == x)
+        def _():
+            wg[core, zh, zl, y, :, self.q] = own[:, 256:640]
+            part = wg.at[core, zh, zl, y, :, self.q]
+            for k in range(1, NZ):
+                to = seq_of(lax.rem(z + k, NZ), y, core)
+                remote(part, part, sems.at[1 + k], sems.at[9 + zh], to, x).start()
+
+        self.pz = []
+        part = wg.at[core, zh, zl, y, :, self.p]
         for k in range(1, NZ):
-            self.now.append(
-                remote(
-                    wg.at[core, z, y], wg.at[core, z, y], sems.at[2 * k], sems.at[2 * k + 1],
-                    seq_of(lax.rem(z + k, NZ), y, core), x,
-                )
+            to = seq_of(lax.rem(z + k, NZ), y, core)
+            self.pz.append(remote(part, part, sems.at[10 + 2 * k], sems.at[11 + 2 * k], to, x))
+        for one in self.pz:
+            one.start()
+
+    def q_along_y(self):
+        seq, x, z, y, core = place()
+        sems, wg = self.sems, self.wg
+        for j in range(2):
+
+            @pl.when(z != x + 4 * j)
+            def _():
+                part = wg.at[core, j, x, y, :, self.q]
+                pltpu.make_async_copy(part, part, sems.at[9 + j]).wait()
+
+        part = wg.at[core, :, x, y, :, self.q]
+        self.qy = []
+        for k in range(1, NY):
+            to = seq_of(z, lax.rem(y + k, NY), core)
+            self.qy.append(remote(part, part, sems.at[26 + 2 * k], sems.at[27 + 2 * k], to, x))
+        for one in self.qy:
+            one.start()
+
+    def p_along_y(self):
+        seq, x, z, y, core = place()
+        sems, wg = self.sems, self.wg
+        for one in self.pz:
+            one.wait()
+        part = wg.at[core, :, :, y, :, self.p]
+        self.py = []
+        for k in range(1, NY):
+            to = seq_of(z, lax.rem(y + k, NY), core)
+            self.py.append(remote(part, part, sems.at[32 + 2 * k], sems.at[33 + 2 * k], to, x))
+        for one in self.py:
+            one.start()
+
+    def q_along_x(self):
+        seq, x, z, y, core = place()
+        sems, wg = self.sems, self.wg
+        for one in self.qy:
+            one.wait()
+        part = wg.at[core, :, x, :, :, self.q]
+        self.qx = []
+        for k in range(1, NX):
+            self.qx.append(
+                remote(part, part, sems.at[38 + 2 * k], sems.at[39 + 2 * k], seq, lax.rem(x + k, NX))
             )
-        self.start()
-
-    def step2(self):
-        seq, x, z, y, core = place()
-        sems, wg = self.sems, self.wg
-        self.wait()
-        self.now = []
-        for k in range(1, NY):
-            self.now.append(
-                remote(
-                    wg.at[core, :, y], wg.at[core, :, y], sems.at[14 + 2 * k], sems.at[15 + 2 * k],
-                    seq_of(z, lax.rem(y + k, NY), core), x,
-                )
-            )
-        self.start()
-
-    def step3(self):
-        seq, x, z, y, core = place()
-        sems, wg = self.sems, self.wg
-        self.wait()
-        self.now = [remote(wg.at[core], wg.at[core], sems.at[22], sems.at[23], seq_of(z, y, 1 - core), x)]
-        self.start()
+        for one in self.qx:
+            one.start()
+
+    def p_pair(self):
+        seq, x, z, y, core = place()
+        for one in self.py:
+            one.wait()
+        part = self.wg.at[core, :, :, :, :, self.p]
+        self.pc = remote(part, part, self.sems.at[46], self.sems.at[47], seq_of(z, y, 1 - core), x)
+        self.pc.start()
+
+    def q_pair(self):
+        seq, x, z, y, core = place()
+        for one in self.qx:
+            one.wait()
+        part = self.wg.at[core, :, :, :, :, self.q]
+        self.qc = remote(part, part, self.sems.at[48], self.sems.at[49], seq_of(z, y, 1 - core), x)
+        self.qc.start()
+
+    def finish(self):
+        seq, x, z, y, core = place()
+        self.pc.wait()
+        self.qc.wait()
+
+        @pl.when(lax.rem(z, 4) == x)
+        def _():
+            part = self.wg.at[core, 0, 0, 0, :, self.q]
+            for k in range(1, NZ):
+                pltpu.make_async_copy(part, part, self.sems.at[1 + k]).wait()
 
 
 class Scatter:
     def __init__(self, at_ref, bg_ref, out, bufs, sems, norm_scale):
         self.at_ref, self.bg_ref, self.out, self.bufs, self.sems = at_ref, bg_ref, out, bufs, sems
         self.norm_scale = norm_scale
+        self.a, self.b = pl.ds(0, 384), pl.ds(384, 256)
 
     def start(self):
         for one in self.now:
@@ -205,7 +269,7 @@
         self.now.append(one)
 
     def product(self):
-        at2, bg2, wsum, wb, xr, s1, wb2, yr, zs, zr, s3 = self.bufs
+        at2, bg2, wsum, wb, xa, yb, sa, sb, wa2, wb2, ya, xb, zs, zr, s3 = self.bufs
         seq, x, z, y, core = place()
         at_ref, bg_ref, sems = self.at_ref, self.bg_ref, self.sems
         mine = pl.multiple_of(core * HALF, 128)
@@ -223,56 +287,77 @@
         self.now = []
         for k in range(1, NX):
             to = lax.rem(x + k, NX)
-            self.now.append(remote(wb.at[to], xr.at[k - 1], sems.at[2 + 2 * k], sems.at[3 + 2 * k], seq, to))
+            self.now.append(
+                remote(wb.at[to, :, :, self.a], xa.at[k - 1], sems.at[2 + 2 * k], sems.at[3 + 2 * k], seq, to)
+            )
+            to = lax.rem(y + k, NY)
+            self.now.append(
+                remote(
+                    wb.at[:, to, :, self.b], yb.at[k - 1], sems.at[8 + 2 * k], sems.at[9 + 2 * k],
+                    seq_of(z, to, core), x,
+                )
+            )
         self.start()
 
-    def after_x(self):
-        at2, bg2, wsum, wb, xr, s1, wb2, yr, zs, zr, s3 = self.bufs
+    def after_one(self):
+        at2, bg2, wsum, wb, xa, yb, sa, sb, wa2, wb2, ya, xb, zs, zr, s3 = self.bufs
         seq, x, z, y, core = place()
         sems = self.sems
         self.wait()
 
-        @pl.loop(0, NY)
+        @pl.loop(0, 4)
         def _(j):
-            total = wsum[x, j]
+            total = wsum[x, j, :, self.a]
             for k in range(3):
-                total += xr[k, j].astype(F32)
-            s1[j] = total
+                total += xa[k, j].astype(F32)
+            sa[j] = total
+            wa2[j] = total.astype(BF16)
+            total = wsum[j, y, :, self.b]
+            for k in range(3):
+                total += yb[k, j].astype(F32)
+            sb[j] = total
             wb2[j] = total.astype(BF16)
 
         self.now = []
         for k in range(1, NY):
             to = lax.rem(y + k, NY)
             self.now.append(
-                remote(wb2.at[to], yr.at[k - 1], sems.at[8 + 2 * k], sems.at[9 + 2 * k], seq_of(z, to, core), x)
+                remote(wa2.at[to], ya.at[k - 1], sems.at[14 + 2 * k], sems.at[15 + 2 * k], seq_of(z, to, core), x)
             )
+            to = lax.rem(x + k, NX)
+            self.now.append(remote(wb2.at[to], xb.at[k - 1], sems.at[20 + 2 * k], sems.at[21 + 2 * k], seq, to))
         self.start()
 
-    def after_y(self):
-        at2, bg2, wsum, wb, xr, s1, wb2, yr, zs, zr, s3 = self.bufs
+    def after_two(self):
+        at2, bg2, wsum, wb, xa, yb, sa, sb, wa2, wb2, ya, xb, zs, zr, s3 = self.bufs
         seq, x, z, y, core = place()
         sems = self.sems
         self.wait()
-        total = s1[y]
+        total = sa[y]
         for k in range(3):
-            total += yr[k].astype(F32)
+            total += ya[k].astype(F32)
+        second = sb[x]
+        for k in range(3):
+            second += xb[k].astype(F32)
 
         def want(r, c):
             low = lax.rem(r, 16)
             return (c == lax.div(r, 16) * 10 + low) & (low < 10)
 
-        zs[...] = matmul(one_hot(128, 80, want), total.astype(BF16)).astype(BF16)
+        chosen = one_hot(128, 80, want)
+        zs[:, self.a] = matmul(chosen, total.astype(BF16)).astype(BF16)
+        zs[:, self.b] = matmul(chosen, second.astype(BF16)).astype(BF16)
         self.now = []
         for k in range(1, NZ):
             to = lax.rem(z + k, NZ)
             src = zs.at[pl.ds(pl.multiple_of(to * 16, 16), 16)]
             self.now.append(
-                remote(src, zr.at[k - 1], sems.at[14 + 2 * k], sems.at[15 + 2 * k], seq_of(to, y, core), x)
+                remote(src, zr.at[k - 1], sems.at[26 + 2 * k], sems.at[27 + 2 * k], seq_of(to, y, core), x)
             )
         self.start()
 
     def after_z(self):
-        at2, bg2, wsum, wb, xr, s1, wb2, yr, zs, zr, s3 = self.bufs
+        zs, zr, s3 = self.bufs[-3:]
         seq, x, z, y, core = place()
         sems, out = self.sems, self.out
         self.wait()
@@ -280,44 +365,32 @@
         for k in range(7):
             total += zr[k].astype(F32)
         s3[...] = total * self.norm_scale
-        owner = 16 * x + 4 * y + lax.div(z, 2)
+        owner = owner_of(x, y, z)
         slot = out.at[lax.rem(z, 2), core]
+        self.now = []
+        for k in range(1, NX):
+            self.now.append(remote(s3, slot, sems.at[41 + k], sems.at[46], owner, lax.rem(x + k, NX)))
+        self.start()
 
         @pl.when(owner != seq)
         def _():
-            remote(s3, slot, sems.at[30], sems.at[31], owner, x).start()
+            remote(s3, slot, sems.at[45], sems.at[46], owner, x).start()
 
         @pl.when(owner == seq)
         def _():
-            pltpu.make_async_copy(s3, slot, sems.at[31]).start()
-
-    def share(self):
+            pltpu.make_async_copy(s3, slot, sems.at[46]).start()
+
+    def finish(self):
         seq, x, z, y, core = place()
         sems, out, s3 = self.sems, self.out, self.bufs[-1]
-        owner = 16 * x + 4 * y + lax.div(z, 2)
-
-        @pl.when(owner != seq)
+        for one in self.now:
+            one.wait_send()
+
+        @pl.when(owner_of(x, y, z) != seq)
         def _():
-            pltpu.make_async_copy(s3, s3, sems.at[30]).wait()
-
-        @pl.when(x == lax.div(seq, 16))
-        def _():
-            pltpu.make_async_copy(out, out, sems.at[31]).wait()
-            for k in range(1, NX):
-                remote(out, out, sems.at[31 + k], sems.at[35], seq, lax.rem(x + k, NX)).start()
-
-    def finish(self):
-        seq, x, z, y, core = place()
-        sems, out = self.sems, self.out
-
-        @pl.when(x == lax.div(seq, 16))
-        def _():
-            for k in range(1, NX):
-                pltpu.make_async_copy(out, out, sems.at[31 + k]).wait()
-
-        @pl.when(x != lax.div(seq, 16))
-        def _():
-            pltpu.make_async_copy(out, out, sems.at[35]).wait()
+            pltpu.make_async_copy(s3, s3, sems.at[45]).wait()
+
+        pltpu.make_async_copy(out, out, sems.at[46]).wait()
 
 
 class GainSum:
@@ -373,7 +446,7 @@
     (x_ref, rowi_ref, coli_ref, gain_ref, gaincol_ref, wqkv_hbm, wout_ref, cot_ref,
      merged_ref, gx_ref, dw_ref, dg_ref,
      wqkv, slots, wg, cslab, crecv, tok, got, xp, normed, kv, projt, eye, perm, permt, probs, at, atp, apad, bg, dat, gt, gn,
-     at2, bg2, wsum, wb, xr, s1, wb2, yr, zs, zr, s3, ghold, g1, g2,
+     at2, bg2, wsum, wb, xa, yb, sa, sb, wa2, wb2, ya, xb, zs, zr, s3, ghold, g1, g2,
      wsem, asem, csend, crecvs, tsend, trecvs, ssem, gsem) = refs
     score_scale = 1.0 / math.sqrt(80)
 
@@ -384,15 +457,16 @@
     for one in loads:
         one.start()
 
+    greet()
+
     def shuffle(r, c):
         return c == lax.rem(r, 4) * 64 + lax.div(r, 4)
 
     stacked = jnp.concatenate([cot_ref[:, pl.ds(c * D, D)] for c in range(4)], axis=0)
     cslab[...] = matmul(one_hot(256, 256, shuffle), stacked).astype(BF16).reshape(SEQ, GROUP, D)
-    greet(True)
+    all_here()
     gather = Gather(wout_ref, slots, wg, asem)
-    gather.step0()
-    exchange_start(cslab, crecv, csend, crecvs)
+    gather.pair()
 
     key_row, key_col = rowi_ref[0:1, :], coli_ref[:, 0:1]
     id_row, id_col = rowi_ref[1:2, :], coli_ref[:, 1:2]
@@ -409,10 +483,13 @@
     centred = wide - jnp.mean(wide, axis=-1, keepdims=True)
     spread = lax.rsqrt(jnp.mean(centred * centred, axis=-1, keepdims=True) + eps)
     normed[...] = (centred * spread * gain_ref[...]).astype(BF16)
-    gather.step1()
+    gather.along_z()
+    exchange_start(cslab, crecv, csend, crecvs)
 
     for j in range(3):
         loads[j].wait()
+        if j == 2:
+            gather.q_along_y()
 
         @pl.loop(0, 5)
         def _(i):
@@ -422,11 +499,10 @@
                 kv[:, pl.ds(pl.multiple_of((j - 1) * D + i * 256, 256), 256)] = part
             projt[cols, :] = matmul_t(eye[...], part).astype(BF16)
 
-    gather.step2()
+    gather.p_along_y()
     same = ids_k == ids_q
 
-    @pl.loop(0, 2)
-    def _(g):
+    def attend(g):
         for h in range(8):
             first, width, off = WINDOWS[h]
             lanes = pl.ds(pl.multiple_of(g * HALF + first, 128), width)
@@ -443,19 +519,23 @@
             padded = jnp.concatenate([part[0:40], gap, part[40:80], gap], axis=0).astype(BF16)
             atp[pl.ds(pl.multiple_of(g * 768 + h * 96, 16), 96), :] = padded
 
-    gather.step3()
+    attend(0)
+    gather.q_along_x()
+    attend(1)
     scatter = Scatter(
-        at, bg, dw_ref, (at2, bg2, wsum, wb, xr, s1, wb2, yr, zs, zr, s3), ssem, norm_scale
+        at, bg, dw_ref, (at2, bg2, wsum, wb, xa, yb, sa, sb, wa2, wb2, ya, xb, zs, zr, s3), ssem, norm_scale
     )
     scatter.send_attended()
     exchange_wait(cslab, crecv, csend, crecvs)
     bg[...] = crecv[...].reshape(256, D)
     scatter.send_grad()
+    gather.p_pair()
     for j in range(6):
         apad[:, pl.ds(j * 256, 256)] = matmul_t(eye[...], atp[pl.ds(j * 256, 256), :]).astype(BF16)
     scatter.product()
 
-    gather.wait()
+    gather.q_pair()
+    gather.finish()
     for half in range(2):
         cols = pl.ds(half * HALF, HALF)
         branch = matmul(apad[...], wg[half].reshape(1536, HALF))
@@ -463,14 +543,13 @@
         tok[:, :, cols] = block.reshape(SEQ, GROUP, HALF)
     exchange_start(tok, got, tsend, trecvs)
 
-    @pl.loop(0, 4)
-    def _(i):
-        part = matmul_t(wg[0, pl.ds(2 * i, 2)].reshape(384, HALF), bg[:, pl.ds(0, HALF)])
-        part += matmul_t(wg[1, pl.ds(2 * i, 2)].reshape(384, HALF), bg[:, pl.ds(HALF, HALF)])
+    for i in range(4):
+        part = matmul_t(wg[0, i // 2, pl.ds(2 * (i % 2), 2)].reshape(384, HALF), bg[:, pl.ds(0, HALF)])
+        part += matmul_t(wg[1, i // 2, pl.ds(2 * (i % 2), 2)].reshape(384, HALF), bg[:, pl.ds(HALF, HALF)])
         for h in range(4):
             own = part[96 * h : 96 * h + 96]
             own = jnp.concatenate([own[0:40], own[48:88]], axis=0).astype(BF16)
-            dat[pl.ds(pl.multiple_of(i * 320 + 80 * h, 16), 80), :] = own
+            dat[pl.ds(i * 320 + 80 * h, 80), :] = own
 
     def back(g):
         for h in range(8):
@@ -487,11 +566,10 @@
             gt[pl.ds(D + rows, 80), :] = matmul_t(projt[pl.ds(rows, 80), :], gs).astype(BF16)
             gt[pl.ds(2 * D + rows, 80), :] = matmul_t(dat[pl.ds(rows, 80), :], low).astype(BF16)
 
-    @pl.loop(0, 2)
-    def _(g):
-        back(g)
-
-    scatter.after_x()
+    back(0)
+    scatter.after_one()
+    back(1)
+    scatter.after_two()
 
     def standard_of(i):
         return matmul_t(eye[...], xp[:, pl.ds(pl.multiple_of(i * 256, 256), 256)])
@@ -528,7 +606,7 @@
     mean_g, mean_gs = lax.fori_loop(0, 5, grads, (zero, zero))
     gains = GainSum(ghold, g1, g2, gsem)
     gains.first(ghold[2])
-    scatter.after_y()
+    scatter.after_z()
     mean_g = mean_g * (1.0 / D)
     mean_gs = mean_gs * (1.0 / D)
 
@@ -541,7 +619,6 @@
         gx_ref[:, rows] = matmul_t(permt[...], total).astype(BF16)
 
     gains.second()
-    scatter.after_z()
     exchange_wait(tok, got, tsend, trecvs)
 
     def unshuffle(r, c):
@@ -551,7 +628,6 @@
     ordered = matmul(unmix, got[...].reshape(256, D)).astype(BF16)
     for c in range(4):
         merged_ref[:, pl.ds(c * D, D)] = ordered[64 * c : 64 * c + 64]
-    scatter.share()
     dg_ref[...] = gains.finish() * norm_scale
     scatter.finish()
 
@@ -584,7 +660,7 @@
         scratch_shapes=[
             pltpu.VMEM((D, 3 * D), BF16),
             pltpu.VMEM((2, 32, D), BF16),
-            pltpu.VMEM((2, NZ, NY, 48, HALF), BF16),
+            pltpu.VMEM((2, 2, 4, NY, 48, HALF), BF16),
             pltpu.VMEM((SEQ, GROUP, D), BF16),
             pltpu.VMEM((SEQ, GROUP, D), BF16),
             pltpu.VMEM((SEQ, GROUP, D), BF16),
@@ -608,10 +684,14 @@
             pltpu.VMEM((256, HALF), BF16),
             pltpu.VMEM((NX, NY, 80, HALF), F32),
             pltpu.VMEM((NX, NY, 80, HALF), BF16),
-            pltpu.VMEM((3, NY, 80, HALF), BF16),
-            pltpu.VMEM((NY, 80, HALF), F32),
-            pltpu.VMEM((NY, 80, HALF), BF16),
-            pltpu.VMEM((3, 80, HALF), BF16),
+            pltpu.VMEM((3, NY, 80, 384), BF16),
+            pltpu.VMEM((3, NX, 80, 256), BF16),
+            pltpu.VMEM((NY, 80, 384), F32),
+            pltpu.VMEM((NX, 80, 256), F32),
+            pltpu.VMEM((NY, 80, 384), BF16),
+            pltpu.VMEM((NX, 80, 256), BF16),
+            pltpu.VMEM((3, 80, 384), BF16),
+            pltpu.VMEM((3, 80, 256), BF16),
             pltpu.VMEM((128, HALF), BF16),
             pltpu.VMEM((7, 16, HALF), BF16),
             pltpu.VMEM((16, HALF), F32),
@@ -619,12 +699,12 @@
             pltpu.VMEM((15, 1, D), F32),
             pltpu.VMEM((15, 1, D), F32),
             pltpu.SemaphoreType.DMA((3,)),
-            pltpu.SemaphoreType.DMA((24,)),
+            pltpu.SemaphoreType.DMA((50,)),
             pltpu.SemaphoreType.DMA,
             pltpu.SemaphoreType.DMA,
             pltpu.SemaphoreType.DMA,
             pltpu.SemaphoreType.DMA,
-            pltpu.SemaphoreType.DMA((36,)),
+            pltpu.SemaphoreType.DMA((47,)),
             pltpu.SemaphoreType.DMA((60,)),
         ],
         compiler_params=pltpu.CompilerParams(

time: 136 us -> 109 us (0.80)
  Pallas kernels: 120 us -> 94.3 us
    pallas_call x1, Pallas kernels: 120 us -> 94.3 us  [per_device(): pl.pallas_call(kernel, out_shape=(jax.ShapeDtypeStruct((SEQ, GROUP * D),...]
where the time goes in v3:
time: 109 us; the launch traced here: 108 us
  Pallas kernels  94.3 us (87%)
  local copies, waits for them, and re-layouts  11 us (10%)
  other arithmetic  2.2 us (2%)
    pallas_call x1, Pallas kernels, per_device(): pl.pallas_call(kernel, out_shape=(jax.ShapeDtypeStruct((SEQ, GROUP * D),...  94.3 us
    unnamed x4, local copies, waits for them, and re-layouts  4.63 us

profile of v3, /device:TPU:1, one launch (start us, length us, event | category | flops | bytes accessed | tf_op | source)
XLA Modules:
  0.0 108.2 jit_solution(14205608745284874116)
XLA Ops:
  0.6 0.7 fusion.2
  1.3 0.1 broadcast_in_dim.11
  1.4 0.1 mul.56
  1.5 0.7 multiply_bitcast_fusion
  2.2 0.2 reduce-window.8
  2.3 0.1 convert_reduce_fusion
  2.4 0.8 copy.18.refs_2_
  3.2 0.1 mul.52
  3.4 0.6 pad_add_fusion.refs_1_
  3.9 1.8 %reshape.130.refs_4_ = f32[1280,1]{1,0:T(8,128)} reshape(f32[1280]{0:T(1024)} %param.10) | data formatting | bytes 10240 | tf_op jit(solution)/shard_map/reshape | solution.py:714
  5.7 1.3 %reshape.127.refs_3_ = f32[1,1280]{1,0:T(1,128)} reshape(f32[1280]{0:T(1024)} %param.10) | data formatting | bytes 10240 | tf_op jit(solution)/shard_map/reshape | solution.py:714
  7.0 94.3 %shard_map.102 = (bf16[64,5120]{1,0:T(8,128)(2,1)}, bf16[256,1280]{1,0:T(8,128)(2,1)}, f32[2,2,16,640]{3,2,1,0:T(8,128)}, f32[1,1280]{1,0:T(1,128)}) custom-call(bf16[256,1280]{1,0:T(8,128)(2,1)} %bitcast.29, s32[2,256]{1,0:T(2,128)} %pad_add_fusion.refs_1_, s32[256,2]{1,0:T(8,128)} %copy.18.refs_2_, f32[1,1280]{1,0:T(1,128)} %reshape.127.refs_3_, ...), custom_call_target="tpu_custom_call" | custom-call | tf_op jit(solution)/shard_map/pallas_call | solution.py:650
  101.3 1.3 %dynamic-slice_bitcast_fusion = f32[20]{0:T(128)} fusion(f32[1,1280]{1,0:T(1,128)} %get-tuple-element.11, s32[]{:T(128)S(6)} %select_n.34), kind=kLoop, calls=%fused_computation.14 | loop fusion | bytes 164 | tf_op jit(solution)/shard_map/dynamic_slice | solution.py:718
  102.6 0.9 slice_bitcast_fusion
  103.5 0.1 copy.20
  103.6 0.7 copy.21
  104.3 2.0 %copy.24 = bf16[1,64,5120]{2,1,0:T(8,128)(2,1)} copy(bf16[1,64,5120]{2,1,0:T(8,128)(2,1)} %bitcast.28) | data formatting | bytes 1310720
  106.3 2.0 %copy.25 = bf16[1,256,1280]{2,1,0:T(8,128)(2,1)} copy(bf16[1,256,1280]{2,1,0:T(8,128)(2,1)} %bitcast.27) | data formatting | bytes 1310720
  (4 shorter events, 0.1 us)

commit v4 on v3

--- a/solution.py
+++ b/solution.py
@@ -102,6 +102,13 @@
 
 def matmul_t(a, b):
     return lax.dot_general(a, b, (((1,), (1,)), ((), ())), preferred_element_type=F32)
+
+
+def three_parts(a):
+    hi = a.astype(BF16)
+    rest = a - hi.astype(F32)
+    mid = rest.astype(BF16)
+    return hi, mid, (rest - mid.astype(F32)).astype(BF16)
 
 
 def one_hot(rows, columns, want):
@@ -443,10 +450,10 @@
 
 
 def kernel_body(norm_scale, refs):
-    (x_ref, rowi_ref, coli_ref, gain_ref, gaincol_ref, wqkv_hbm, wout_ref, cot_ref,
-     merged_ref, gx_ref, dw_ref, dg_ref,
-     wqkv, slots, wg, cslab, crecv, tok, got, xp, normed, kv, projt, eye, perm, permt, probs, at, atp, apad, bg, dat, gt, gn,
-     at2, bg2, wsum, wb, xa, yb, sa, sb, wa2, wb2, ya, xb, zs, zr, s3, ghold, g1, g2,
+    (x_ref, dest_ref, len_ref, gain_ref, wqkv_hbm, wout_ref, cot_ref,
+     got, gx_ref, dw_ref, dg_ref,
+     wqkv, slots, wg, cslab, crecv, tok, xp, normed, kv, projt, eye, perm, permt, probs, at, atp, apad, bg, dat, gt, gn,
+     at2, bg2, wsum, wb, xa, yb, sa, sb, wa2, wb2, ya, xb, zs, zr, s3, ghold, g1, g2, gaincol,
      wsem, asem, csend, crecvs, tsend, trecvs, ssem, gsem) = refs
     score_scale = 1.0 / math.sqrt(80)
 
@@ -468,21 +475,32 @@
     gather = Gather(wout_ref, slots, wg, asem)
     gather.pair()
 
-    key_row, key_col = rowi_ref[0:1, :], coli_ref[:, 0:1]
-    id_row, id_col = rowi_ref[1:2, :], coli_ref[:, 1:2]
+    slot = jnp.broadcast_to(lax.shift_right_logical(dest_ref[...], 6), (8, 64)).astype(F32).astype(BF16)
+    to_row = matmul(slot, one_hot(64, 256, lambda r, c: r == lax.div(c, 4)))[0:1]
+    to_col = matmul_t(one_hot(256, 64, lambda r, c: c == lax.div(r, 4)), slot)[:, 0:1]
+    row_number = lax.broadcasted_iota(jnp.int32, (1, 256), 1)
+    col_number = lax.broadcasted_iota(jnp.int32, (256, 1), 0)
+    key_row = to_row.astype(jnp.int32) * GROUP + lax.rem(row_number, GROUP)
+    key_col = to_col.astype(jnp.int32) * GROUP + lax.rem(col_number, GROUP)
+    id_row, id_col = jnp.zeros((1, 256), F32), jnp.zeros((256, 1), F32)
+    end = 0
+    for j in range(3):
+        end = end + len_ref[0, j] * GROUP
+        id_row += jnp.where(row_number >= end, 1.0, 0.0)
+        id_col += jnp.where(col_number >= end, 1.0, 0.0)
     ir = lax.broadcasted_iota(jnp.int32, (256, 256), 0)
     ic = lax.broadcasted_iota(jnp.int32, (256, 256), 1)
     eye[...] = jnp.where(ir == ic, 1.0, 0.0).astype(BF16)
     perm[...] = jnp.where(ir == key_row, 1.0, 0.0).astype(BF16)
     permt[...] = jnp.where(ic == key_col, 1.0, 0.0).astype(BF16)
-    ids_k = jnp.sum(jnp.where(ir == key_row, id_row.astype(F32), 0.0), axis=1, keepdims=True)
-    ids_q = jnp.sum(jnp.where(ic == key_col, id_col.astype(F32), 0.0), axis=0, keepdims=True)
+    ids_k = jnp.sum(jnp.where(ir == key_row, id_row, 0.0), axis=1, keepdims=True)
+    ids_q = jnp.sum(jnp.where(ic == key_col, id_col, 0.0), axis=0, keepdims=True)
 
     wide = matmul(perm[...], x_ref[...])
     xp[...] = wide.astype(BF16)
     centred = wide - jnp.mean(wide, axis=-1, keepdims=True)
     spread = lax.rsqrt(jnp.mean(centred * centred, axis=-1, keepdims=True) + eps)
-    normed[...] = (centred * spread * gain_ref[...]).astype(BF16)
+    normed[...] = (centred * spread * gain_ref[...].reshape(1, D)).astype(BF16)
     gather.along_z()
     exchange_start(cslab, crecv, csend, crecvs)
 
@@ -534,6 +552,15 @@
         apad[:, pl.ds(j * 256, 256)] = matmul_t(eye[...], atp[pl.ds(j * 256, 256), :]).astype(BF16)
     scatter.product()
 
+
+    @pl.loop(0, 5)
+    def _(i):
+        rows = pl.ds(pl.multiple_of(i * 256, 256), 256)
+        total = jnp.zeros((256, 256), F32)
+        for part in three_parts(gain_ref[rows].reshape(1, 256)):
+            total += matmul_t(eye[...], jnp.broadcast_to(part, (256, 256)))
+        gaincol[rows, :] = total
+
     gather.q_pair()
     gather.finish()
     for half in range(2):
@@ -590,14 +617,11 @@
         part = matmul(wqkv[rows, :], gt[...])
         std = (standard_of(i) - mean) * inv
         both = part * std
-        hi = both.astype(BF16)
-        rest = both - hi.astype(F32)
-        mid = rest.astype(BF16)
-        lo = (rest - mid.astype(F32)).astype(BF16)
         ones = jnp.ones((8, 256), BF16)
+        hi, mid, lo = three_parts(both)
         row = matmul_t(ones, hi) + matmul_t(ones, mid) + matmul_t(ones, lo)
         ghold[2, :, rows] = row[0:1]
-        scaled = part * gaincol_ref[rows, :]
+        scaled = part * gaincol[rows, :]
         gn[rows, :] = scaled
         a, b = carry
         return (a + jnp.sum(scaled, axis=0, keepdims=True), b + jnp.sum(scaled * std, axis=0, keepdims=True))
@@ -621,47 +645,48 @@
     gains.second()
     exchange_wait(tok, got, tsend, trecvs)
 
-    def unshuffle(r, c):
-        return r == lax.rem(c, 4) * 64 + lax.div(c, 4)
-
-    unmix = one_hot(256, 256, unshuffle)
-    ordered = matmul(unmix, got[...].reshape(256, D)).astype(BF16)
+    dg_ref[...] = gains.finish() * norm_scale
+    scatter.finish()
+
+
+def finish_kernel(got_ref, gx_in, dw_ref, dg_ref, merged_ref, gx_ref, own_ref, gain_out):
+    ordered = matmul(
+        one_hot(256, 256, lambda r, c: r == lax.rem(c, 4) * 64 + lax.div(c, 4)), got_ref[...].reshape(256, D)
+    ).astype(BF16)
     for c in range(4):
         merged_ref[:, pl.ds(c * D, D)] = ordered[64 * c : 64 * c + 64]
-    dg_ref[...] = gains.finish() * norm_scale
-    scatter.finish()
+    gx_ref[...] = gx_in[...]
+    for part in range(2):
+        for core in range(2):
+            own_ref[pl.ds(10 * part, 10), pl.ds(core * HALF, HALF)] = dw_ref[part, core, 0:10, :]
+    first = lax.axis_index("seq") * 20
+    turned = pltpu.roll(jnp.broadcast_to(dg_ref[...], (8, D)), lax.rem(D - first, D), 1)
+    gain_out[...] = turned[0, 0:20]
 
 
 def per_device(patches, lengths, token_dest, gain, w_qkv, w_out, cotangent):
     norm_scale = 1.0 / math.sqrt(256 * SEQ * NX)
-    row = jnp.arange(256, dtype=jnp.int32)
-    slot = jnp.repeat(token_dest[0] // 64, GROUP)
-    key = slot * GROUP + row % GROUP
-    ends = jnp.cumsum(lengths[0, 0] * GROUP)
-    ids = jnp.sum((row[:, None] >= ends[None, :]).astype(jnp.int32), axis=1)
-    rows = jnp.stack([key, ids])
-    columns = jnp.stack([key, ids], axis=1)
     vmem = pl.BlockSpec(memory_space=pltpu.VMEM)
     hbm = pl.BlockSpec(memory_space=pl.ANY)
+    smem = pl.BlockSpec(memory_space=pltpu.SMEM)
 
     def kernel(*refs):
         kernel_body(norm_scale, refs)
 
-    merged, gx, dw, dg = pl.pallas_call(
+    got, gx, dw, dg = pl.pallas_call(
         kernel,
         out_shape=(
-            jax.ShapeDtypeStruct((SEQ, GROUP * D), BF16),
+            jax.ShapeDtypeStruct((SEQ, GROUP, D), BF16),
             jax.ShapeDtypeStruct((256, D), BF16),
             jax.ShapeDtypeStruct((2, 2, 16, HALF), F32),
             jax.ShapeDtypeStruct((1, D), F32),
         ),
-        in_specs=[vmem] * 5 + [hbm] + [vmem] * 2,
+        in_specs=[vmem, vmem, smem, vmem, hbm, vmem, vmem],
         out_specs=(vmem,) * 4,
         scratch_shapes=[
             pltpu.VMEM((D, 3 * D), BF16),
             pltpu.VMEM((2, 32, D), BF16),
             pltpu.VMEM((2, 2, 4, NY, 48, HALF), BF16),
-            pltpu.VMEM((SEQ, GROUP, D), BF16),
             pltpu.VMEM((SEQ, GROUP, D), BF16),
             pltpu.VMEM((SEQ, GROUP, D), BF16),
             pltpu.VMEM((SEQ, GROUP, D), BF16),
@@ -698,6 +723,7 @@
             pltpu.VMEM((3, 1, D), F32),
             pltpu.VMEM((15, 1, D), F32),
             pltpu.VMEM((15, 1, D), F32),
+            pltpu.VMEM((D, 256), F32),
             pltpu.SemaphoreType.DMA((3,)),
             pltpu.SemaphoreType.DMA((50,)),
             pltpu.SemaphoreType.DMA,
@@ -711,11 +737,20 @@
             collective_id=0, has_side_effects=True, vmem_limit_bytes=LIMIT
         ),
     )(
-        patches[0], rows, columns, gain.reshape(1, D), gain.reshape(D, 1), w_qkv, w_out,
-        cotangent[0],
+        patches[0], token_dest, lengths[0], gain, w_qkv, w_out, cotangent[0],
     )
-    own_weight = jnp.transpose(dw[:, :, :10], (0, 2, 1, 3)).reshape(20, D)
-    own_gain = lax.dynamic_slice_in_dim(dg.reshape(D), lax.axis_index("seq") * 20, 20, 0)
+    merged, gx, own_weight, own_gain = pl.pallas_call(
+        finish_kernel,
+        out_shape=(
+            jax.ShapeDtypeStruct((SEQ, GROUP * D), BF16),
+            jax.ShapeDtypeStruct((256, D), BF16),
+            jax.ShapeDtypeStruct((20, D), F32),
+            jax.ShapeDtypeStruct((20,), F32),
+        ),
+        in_specs=[vmem] * 4,
+        out_specs=(vmem,) * 4,
+        compiler_params=pltpu.CompilerParams(vmem_limit_bytes=2**24),
+    )(got, gx, dw, dg)
     return (merged[None], gx[None], own_weight, own_gain)
 
 

time: 109 us -> 99.9 us (0.917)
  local copies, waits for them, and re-layouts: 11 us -> 3.77 us
  other arithmetic: 2.2 us -> 0 us
    reshape x2 -> x0, local copies, waits for them, and re-layouts: 3.06 us -> none  [the longest x1 1.77 us: per_device(): gain.reshape(D, 1)]
    mul x2 -> x0, other arithmetic: 1.33 us -> none  [the longest x1 0.67 us: per_device(): key = slot * GROUP + row % GROUP]
    dynamic_slice x1 -> x0, local copies, waits for them, and re-layouts: 1.26 us -> none  [per_device(): lax.dynamic_slice_in_dim(dg.reshape(D), lax.axis_index('seq') * 20, 20, 0)]
    pallas_call x1 -> x2, Pallas kernels: 94.3 us -> 95.2 us  [the longest x1 93.8 us: per_device(): pl.pallas_call(kernel, out_shape=(jax.ShapeDtypeStruct((SEQ, GROUP, D), B...]
    unnamed x4 -> x8, local copies, waits for them, and re-layouts: 4.63 us -> 3.77 us
where the time goes in v4:
time: 99.9 us; the launch traced here: 99.6 us
  Pallas kernels  95.2 us (95%)
  local copies, waits for them, and re-layouts  3.77 us (4%)
    pallas_call x1, Pallas kernels, per_device(): pl.pallas_call(kernel, out_shape=(jax.ShapeDtypeStruct((SEQ, GROUP, D), B...  93.8 us
    unnamed x8, local copies, waits for them, and re-layouts  3.77 us

profile of v4, /device:TPU:1, one launch (start us, length us, event | category | flops | bytes accessed | tf_op | source)
XLA Modules:
  0.0 99.6 jit_solution(17503794130529053186)
XLA Ops:
  0.6 93.8 %shard_map.102 = (bf16[64,4,1280]{2,1,0:T(4,128)(2,1)}, bf16[256,1280]{1,0:T(8,128)(2,1)}, f32[2,2,16,640]{3,2,1,0:T(8,128)}, f32[1,1280]{1,0:T(1,128)}) custom-call(bf16[256,1280]{1,0:T(8,128)(2,1)} %bitcast.5, s32[1,64]{1,0:T(1,128)} %refs_1_.1, s32[1,4]{1,0:T(1,128)} %bitcast.7, f32[1280]{0:T(1024)} %refs_3_.1, bf16[1280,3840]{1,0:T(8,128)(2,1)} %refs_4_.1, ...), custom_call_target="tpu_custom_call" | custom-call | tf_op jit(solution)/shard_map/pallas_call | solution.py:676
  94.4 0.0 copy-start
  94.5 1.1 %copy-done = bf16[64,4,1280]{2,1,0:T(4,128)(2,1)S(1)} copy-done((bf16[64,4,1280]{2,1,0:T(4,128)(2,1)S(1)}, bf16[64,4,1280]{2,1,0:T(4,128)(2,1)}, u32[]{:S(2)}) %copy-start) | copy-done | bytes 655384
  95.5 0.0 copy-start.1
  95.5 1.1 %copy-done.1 = bf16[256,1280]{1,0:T(8,128)(2,1)S(1)} copy-done((bf16[256,1280]{1,0:T(8,128)(2,1)S(1)}, bf16[256,1280]{1,0:T(8,128)(2,1)}, u32[]{:S(2)}) %copy-start.1) | copy-done | bytes 655384
  96.6 0.0 copy-start.2
  96.6 0.9 copy-done.2
  97.5 0.0 copy-start.3
  97.5 0.7 copy-done.3
  98.2 1.4 %shard_map.103 = (bf16[64,5120]{1,0:T(8,128)(2,1)}, bf16[256,1280]{1,0:T(8,128)(2,1)}, f32[20,1280]{1,0:T(8,128)}, f32[20]{0:T(128)}) custom-call(bf16[64,4,1280]{2,1,0:T(4,128)(2,1)S(1)} %copy-done, bf16[256,1280]{1,0:T(8,128)(2,1)S(1)} %copy-done.1, f32[2,2,16,640]{3,2,1,0:T(8,128)S(1)} %copy-done.2, f32[1,1280]{1,0:T(1,128)S(1)} %copy-done.3), custom_call_target="tpu_custom_call" | custom-call | tf_op jit(solution)/shard_map/pallas_call | solution.py:742
Async XLA Ops:
  94.4 1.1 %copy-start = (bf16[64,4,1280]{2,1,0:T(4,128)(2,1)S(1)}, bf16[64,4,1280]{2,1,0:T(4,128)(2,1)}, u32[]{:S(2)}) copy-start(bf16[64,4,1280]{2,1,0:T(4,128)(2,1)} %get-tuple-element.12.got_ref) | copy-start | bytes 1966084
  95.5 1.1 %copy-start.1 = (bf16[256,1280]{1,0:T(8,128)(2,1)S(1)}, bf16[256,1280]{1,0:T(8,128)(2,1)}, u32[]{:S(2)}) copy-start(bf16[256,1280]{1,0:T(8,128)(2,1)} %get-tuple-element.13.gx_in) | copy-start | bytes 1966084
  96.6 0.9 copy-start.2
  97.5 0.7 copy-start.3

commit v5 on v4

--- a/solution.py
+++ b/solution.py
@@ -104,11 +104,13 @@
     return lax.dot_general(a, b, (((1,), (1,)), ((), ())), preferred_element_type=F32)
 
 
-def three_parts(a):
-    hi = a.astype(BF16)
-    rest = a - hi.astype(F32)
-    mid = rest.astype(BF16)
-    return hi, mid, (rest - mid.astype(F32)).astype(BF16)
+class Pool:
+    def __init__(self, sems):
+        self.sems, self.used = sems, 0
+
+    def take(self):
+        self.used += 1
+        return self.sems.at[self.used - 1]
 
 
 def one_hot(rows, columns, want):
@@ -131,20 +133,25 @@
 
 class Gather:
     def __init__(self, w_ref, slots, wg, sems):
-        self.w_ref, self.slots, self.wg, self.sems = w_ref, slots, wg, sems
+        self.w_ref, self.slots, self.wg = w_ref, slots, wg
+        self.pool = Pool(sems)
         self.p, self.q = pl.ds(0, 256), pl.ds(256, 384)
 
+    def send(self, part, to, x):
+        one = remote(part, part, self.pool.take(), self.pool.take(), to, x)
+        one.start()
+        return one
+
     def pair(self):
         seq, x, z, y, core = place()
-        slots, sems = self.slots, self.sems
+        slots = self.slots
         own = jnp.concatenate([self.w_ref[...].astype(F32), jnp.zeros((12, D), F32)], axis=0)
         slots[core] = own.astype(BF16)
-        self.first = remote(slots.at[core], slots.at[core], sems.at[0], sems.at[1], seq_of(z, y, 1 - core), x)
-        self.first.start()
+        self.first = self.send(slots.at[core], seq_of(z, y, 1 - core), x)
 
     def along_z(self):
         seq, x, z, y, core = place()
-        slots, sems, wg = self.slots, self.sems, self.wg
+        slots, wg = self.slots, self.wg
         zh, zl = lax.div(z, 4), lax.rem(z, 4)
         self.first.wait()
 
@@ -155,6 +162,9 @@
         rows = jnp.concatenate([slots[0, :, pl.ds(first, HALF)], slots[1, :, pl.ds(first, HALF)]], axis=0)
         own = matmul(one_hot(48, 64, want), rows).astype(BF16)
         wg[core, zh, zl, y, :, self.p] = own[:, 0:256]
+        self.zsend = [self.pool.take() for _ in range(1, NZ)]
+        both = self.pool.used
+        self.zrecv = [self.pool.take() for _ in range(2)]
 
         @pl.when(zl == x)
         def _():
@@ -162,154 +172,124 @@
             part = wg.at[core, zh, zl, y, :, self.q]
             for k in range(1, NZ):
                 to = seq_of(lax.rem(z + k, NZ), y, core)
-                remote(part, part, sems.at[1 + k], sems.at[9 + zh], to, x).start()
-
-        self.pz = []
+                remote(part, part, self.zsend[k - 1], self.pool.sems.at[both + zh], to, x).start()
+
         part = wg.at[core, zh, zl, y, :, self.p]
-        for k in range(1, NZ):
-            to = seq_of(lax.rem(z + k, NZ), y, core)
-            self.pz.append(remote(part, part, sems.at[10 + 2 * k], sems.at[11 + 2 * k], to, x))
-        for one in self.pz:
-            one.start()
+        self.pz = [self.send(part, seq_of(lax.rem(z + k, NZ), y, core), x) for k in range(1, NZ)]
+
+    def q_forward(self, k):
+        seq, x, z, y, core = place()
+        part = self.wg.at[core, :, x, lax.rem(y + NY - k, NY), :, self.q]
+        self.qx.append([self.send(part, seq, lax.rem(x + j, NX)) for j in range(1, NX)])
 
     def q_along_y(self):
         seq, x, z, y, core = place()
-        sems, wg = self.sems, self.wg
+        wg = self.wg
         for j in range(2):
 
             @pl.when(z != x + 4 * j)
             def _():
                 part = wg.at[core, j, x, y, :, self.q]
-                pltpu.make_async_copy(part, part, sems.at[9 + j]).wait()
+                pltpu.make_async_copy(part, part, self.zrecv[j]).wait()
 
         part = wg.at[core, :, x, y, :, self.q]
-        self.qy = []
-        for k in range(1, NY):
-            to = seq_of(z, lax.rem(y + k, NY), core)
-            self.qy.append(remote(part, part, sems.at[26 + 2 * k], sems.at[27 + 2 * k], to, x))
-        for one in self.qy:
-            one.start()
+        self.qy = [self.send(part, seq_of(z, lax.rem(y + k, NY), core), x) for k in range(1, NY)]
+        self.qx = []
+        self.q_forward(0)
+
+    def p_to_pair(self, k):
+        seq, x, z, y, core = place()
+        part = self.wg.at[core, :, :, lax.rem(y + NY - k, NY), :, self.p]
+        self.last.append(self.send(part, seq_of(z, y, 1 - core), x))
 
     def p_along_y(self):
         seq, x, z, y, core = place()
-        sems, wg = self.sems, self.wg
         for one in self.pz:
             one.wait()
-        part = wg.at[core, :, :, y, :, self.p]
-        self.py = []
+        part = self.wg.at[core, :, :, y, :, self.p]
+        self.py = [self.send(part, seq_of(z, lax.rem(y + k, NY), core), x) for k in range(1, NY)]
+        self.last = []
+        self.p_to_pair(0)
+
+    def q_along_x(self):
         for k in range(1, NY):
-            to = seq_of(z, lax.rem(y + k, NY), core)
-            self.py.append(remote(part, part, sems.at[32 + 2 * k], sems.at[33 + 2 * k], to, x))
-        for one in self.py:
-            one.start()
-
-    def q_along_x(self):
-        seq, x, z, y, core = place()
-        sems, wg = self.sems, self.wg
-        for one in self.qy:
+            self.qy[k - 1].wait()
+            self.q_forward(k)
+
+    def p_pair(self):
+        for k in range(1, NY):
+            self.py[k - 1].wait()
+            self.p_to_pair(k)
+
+    def q_pair(self):
+        seq, x, z, y, core = place()
+        for k in range(NY):
+            for one in self.qx[k]:
+                one.wait()
+            part = self.wg.at[core, :, :, lax.rem(y + NY - k, NY), :, self.q]
+            self.last.append(self.send(part, seq_of(z, y, 1 - core), x))
+
+    def finish(self):
+        seq, x, z, y, core = place()
+        for one in self.last:
             one.wait()
-        part = wg.at[core, :, x, :, :, self.q]
-        self.qx = []
-        for k in range(1, NX):
-            self.qx.append(
-                remote(part, part, sems.at[38 + 2 * k], sems.at[39 + 2 * k], seq, lax.rem(x + k, NX))
-            )
-        for one in self.qx:
-            one.start()
-
-    def p_pair(self):
-        seq, x, z, y, core = place()
-        for one in self.py:
-            one.wait()
-        part = self.wg.at[core, :, :, :, :, self.p]
-        self.pc = remote(part, part, self.sems.at[46], self.sems.at[47], seq_of(z, y, 1 - core), x)
-        self.pc.start()
-
-    def q_pair(self):
-        seq, x, z, y, core = place()
-        for one in self.qx:
-            one.wait()
-        part = self.wg.at[core, :, :, :, :, self.q]
-        self.qc = remote(part, part, self.sems.at[48], self.sems.at[49], seq_of(z, y, 1 - core), x)
-        self.qc.start()
-
-    def finish(self):
-        seq, x, z, y, core = place()
-        self.pc.wait()
-        self.qc.wait()
 
         @pl.when(lax.rem(z, 4) == x)
         def _():
             part = self.wg.at[core, 0, 0, 0, :, self.q]
             for k in range(1, NZ):
-                pltpu.make_async_copy(part, part, self.sems.at[1 + k]).wait()
+                pltpu.make_async_copy(part, part, self.zsend[k - 1]).wait()
 
 
 class Scatter:
     def __init__(self, at_ref, bg_ref, out, bufs, sems, norm_scale):
         self.at_ref, self.bg_ref, self.out, self.bufs, self.sems = at_ref, bg_ref, out, bufs, sems
+        self.pool = Pool(sems)
         self.norm_scale = norm_scale
         self.a, self.b = pl.ds(0, 384), pl.ds(384, 256)
-
-    def start(self):
-        for one in self.now:
-            one.start()
 
     def wait(self):
         for one in self.now:
             one.wait()
 
+    def send(self, src, dst, to, x):
+        one = remote(src, dst, self.pool.take(), self.pool.take(), to, x)
+        one.start()
+        return one
+
     def send_attended(self):
         seq, x, z, y, core = place()
-        partner = seq_of(z, y, 1 - core)
-        self.now = [remote(self.at_ref, self.bufs[0], self.sems.at[0], self.sems.at[1], partner, x)]
-        self.now[0].start()
+        at = self.at_ref
+        self.now = [self.send(at.at[:, pl.ds(0, 256)], at.at[:, pl.ds(256, 256)], seq_of(z, y, 1 - core), x)]
 
     def send_grad(self):
         seq, x, z, y, core = place()
-        partner = seq_of(z, y, 1 - core)
+        pair = self.bufs[0]
         theirs = pl.multiple_of((1 - core) * HALF, 128)
-        one = remote(
-            self.bg_ref.at[:, pl.ds(theirs, HALF)], self.bufs[1], self.sems.at[2], self.sems.at[3], partner, x
-        )
-        one.start()
-        self.now.append(one)
+        src = self.bg_ref.at[:, pl.ds(theirs, HALF)]
+        self.now.append(self.send(src, pair.at[pl.ds(256, 256)], seq_of(z, y, 1 - core), x))
+        pair[pl.ds(0, 256), :] = self.bg_ref[:, pl.ds(pl.multiple_of(core * HALF, 128), HALF)]
 
     def product(self):
-        at2, bg2, wsum, wb, xa, yb, sa, sb, wa2, wb2, ya, xb, zs, zr, s3 = self.bufs
-        seq, x, z, y, core = place()
-        at_ref, bg_ref, sems = self.at_ref, self.bg_ref, self.sems
-        mine = pl.multiple_of(core * HALF, 128)
+        pair, wsum, wb, xa, yb, sa, sb, wa2, wb2, ya, xb, zs, zr, s3 = self.bufs
+        seq, x, z, y, core = place()
         self.wait()
-
-        @pl.loop(0, NX)
-        def _(i):
+        self.now = []
+        for k in (1, 2, 3, 0):
+            i = lax.rem(x + k, NX)
             rows = pl.ds(pl.multiple_of(i * 320, 64), 320)
-            part = matmul(at_ref[rows, :], bg_ref[:, pl.ds(mine, HALF)])
-            part += matmul(at2[rows, :], bg2[...])
-            part = part.reshape(NY, 80, HALF)
+            part = matmul(self.at_ref[rows, :], pair[...]).reshape(NY, 80, HALF)
             wsum[i] = part
             wb[i] = part.astype(BF16)
-
-        self.now = []
-        for k in range(1, NX):
-            to = lax.rem(x + k, NX)
-            self.now.append(
-                remote(wb.at[to, :, :, self.a], xa.at[k - 1], sems.at[2 + 2 * k], sems.at[3 + 2 * k], seq, to)
-            )
-            to = lax.rem(y + k, NY)
-            self.now.append(
-                remote(
-                    wb.at[:, to, :, self.b], yb.at[k - 1], sems.at[8 + 2 * k], sems.at[9 + 2 * k],
-                    seq_of(z, to, core), x,
-                )
-            )
-        self.start()
+            if k > 0:
+                self.now.append(self.send(wb.at[i, :, :, self.a], xa.at[k - 1], seq, i))
+            for j in range(1, NY):
+                to = lax.rem(y + j, NY)
+                self.now.append(self.send(wb.at[i, to, :, self.b], yb.at[j - 1, i], seq_of(z, to, core), x))
 
     def after_one(self):
-        at2, bg2, wsum, wb, xa, yb, sa, sb, wa2, wb2, ya, xb, zs, zr, s3 = self.bufs
-        seq, x, z, y, core = place()
-        sems = self.sems
+        pair, wsum, wb, xa, yb, sa, sb, wa2, wb2, ya, xb, zs, zr, s3 = self.bufs
+        seq, x, z, y, core = place()
         self.wait()
 
         @pl.loop(0, 4)
@@ -328,17 +308,13 @@
         self.now = []
         for k in range(1, NY):
             to = lax.rem(y + k, NY)
-            self.now.append(
-                remote(wa2.at[to], ya.at[k - 1], sems.at[14 + 2 * k], sems.at[15 + 2 * k], seq_of(z, to, core), x)
-            )
+            self.now.append(self.send(wa2.at[to], ya.at[k - 1], seq_of(z, to, core), x))
             to = lax.rem(x + k, NX)
-            self.now.append(remote(wb2.at[to], xb.at[k - 1], sems.at[20 + 2 * k], sems.at[21 + 2 * k], seq, to))
-        self.start()
+            self.now.append(self.send(wb2.at[to], xb.at[k - 1], seq, to))
 
     def after_two(self):
-        at2, bg2, wsum, wb, xa, yb, sa, sb, wa2, wb2, ya, xb, zs, zr, s3 = self.bufs
-        seq, x, z, y, core = place()
-        sems = self.sems
+        pair, wsum, wb, xa, yb, sa, sb, wa2, wb2, ya, xb, zs, zr, s3 = self.bufs
+        seq, x, z, y, core = place()
         self.wait()
         total = sa[y]
         for k in range(3):
@@ -358,15 +334,12 @@
         for k in range(1, NZ):
             to = lax.rem(z + k, NZ)
             src = zs.at[pl.ds(pl.multiple_of(to * 16, 16), 16)]
-            self.now.append(
-                remote(src, zr.at[k - 1], sems.at[26 + 2 * k], sems.at[27 + 2 * k], seq_of(to, y, core), x)
-            )
-        self.start()
+            self.now.append(self.send(src, zr.at[k - 1], seq_of(to, y, core), x))
 
     def after_z(self):
         zs, zr, s3 = self.bufs[-3:]
         seq, x, z, y, core = place()
-        sems, out = self.sems, self.out
+        out = self.out
         self.wait()
         total = zs[pl.ds(pl.multiple_of(z * 16, 16), 16), :].astype(F32)
         for k in range(7):
@@ -374,30 +347,32 @@
         s3[...] = total * self.norm_scale
         owner = owner_of(x, y, z)
         slot = out.at[lax.rem(z, 2), core]
-        self.now = []
-        for k in range(1, NX):
-            self.now.append(remote(s3, slot, sems.at[41 + k], sems.at[46], owner, lax.rem(x + k, NX)))
-        self.start()
+        self.sent, self.got = self.pool.take(), self.pool.take()
+        self.now = [
+            remote(s3, slot, self.pool.take(), self.got, owner, lax.rem(x + k, NX)) for k in range(1, NX)
+        ]
+        for one in self.now:
+            one.start()
 
         @pl.when(owner != seq)
         def _():
-            remote(s3, slot, sems.at[45], sems.at[46], owner, x).start()
+            remote(s3, slot, self.sent, self.got, owner, x).start()
 
         @pl.when(owner == seq)
         def _():
-            pltpu.make_async_copy(s3, slot, sems.at[46]).start()
+            pltpu.make_async_copy(s3, slot, self.got).start()
 
     def finish(self):
         seq, x, z, y, core = place()
-        sems, out, s3 = self.sems, self.out, self.bufs[-1]
+        out, s3 = self.out, self.bufs[-1]
         for one in self.now:
             one.wait_send()
 
         @pl.when(owner_of(x, y, z) != seq)
         def _():
-            pltpu.make_async_copy(s3, s3, sems.at[45]).wait()
-
-        pltpu.make_async_copy(out, out, sems.at[46]).wait()
+            pltpu.make_async_copy(s3, s3, self.sent).wait()
+
+        pltpu.make_async_copy(out, out, self.got).wait()
 
 
 class GainSum:
@@ -452,8 +427,8 @@
 def kernel_body(norm_scale, refs):
     (x_ref, dest_ref, len_ref, gain_ref, wqkv_hbm, wout_ref, cot_ref,
      got, gx_ref, dw_ref, dg_ref,
-     wqkv, slots, wg, cslab, crecv, tok, xp, normed, kv, projt, eye, perm, permt, probs, at, atp, apad, bg, dat, gt, gn,
-     at2, bg2, wsum, wb, xa, yb, sa, sb, wa2, wb2, ya, xb, zs, zr, s3, ghold, g1, g2, gaincol,
+     wqkv, slots, wg, cslab, crecv, tok, xp, normed, kv, projt, permt, probs, at, atp, apad, bg, bgt, dat, gt, gn, std, pair,
+     wsum, wb, xa, yb, sa, sb, wa2, wb2, ya, xb, zs, zr, s3, ghold, g1, g2, gaincol,
      wsem, asem, csend, crecvs, tsend, trecvs, ssem, gsem) = refs
     score_scale = 1.0 / math.sqrt(80)
 
@@ -471,10 +446,6 @@
 
     stacked = jnp.concatenate([cot_ref[:, pl.ds(c * D, D)] for c in range(4)], axis=0)
     cslab[...] = matmul(one_hot(256, 256, shuffle), stacked).astype(BF16).reshape(SEQ, GROUP, D)
-    all_here()
-    gather = Gather(wout_ref, slots, wg, asem)
-    gather.pair()
-
     slot = jnp.broadcast_to(lax.shift_right_logical(dest_ref[...], 6), (8, 64)).astype(F32).astype(BF16)
     to_row = matmul(slot, one_hot(64, 256, lambda r, c: r == lax.div(c, 4)))[0:1]
     to_col = matmul_t(one_hot(256, 64, lambda r, c: c == lax.div(r, 4)), slot)[:, 0:1]
@@ -490,33 +461,35 @@
         id_col += jnp.where(col_number >= end, 1.0, 0.0)
     ir = lax.broadcasted_iota(jnp.int32, (256, 256), 0)
     ic = lax.broadcasted_iota(jnp.int32, (256, 256), 1)
-    eye[...] = jnp.where(ir == ic, 1.0, 0.0).astype(BF16)
-    perm[...] = jnp.where(ir == key_row, 1.0, 0.0).astype(BF16)
+    perm = jnp.where(ir == key_row, 1.0, 0.0).astype(BF16)
     permt[...] = jnp.where(ic == key_col, 1.0, 0.0).astype(BF16)
     ids_k = jnp.sum(jnp.where(ir == key_row, id_row, 0.0), axis=1, keepdims=True)
     ids_q = jnp.sum(jnp.where(ic == key_col, id_col, 0.0), axis=0, keepdims=True)
 
-    wide = matmul(perm[...], x_ref[...])
+    wide = matmul(perm, x_ref[...])
     xp[...] = wide.astype(BF16)
     centred = wide - jnp.mean(wide, axis=-1, keepdims=True)
     spread = lax.rsqrt(jnp.mean(centred * centred, axis=-1, keepdims=True) + eps)
     normed[...] = (centred * spread * gain_ref[...].reshape(1, D)).astype(BF16)
+
+    all_here()
+    gather = Gather(wout_ref, slots, wg, asem)
+    gather.pair()
+
+    def project(j):
+        loads[j].wait()
+        cols = pl.ds(j * D, D)
+        part = matmul(normed[...], wqkv[:, cols]).astype(BF16)
+        if j > 0:
+            kv[:, pl.ds((j - 1) * D, D)] = part
+        projt[cols, :] = part.T
+
+    project(0)
     gather.along_z()
     exchange_start(cslab, crecv, csend, crecvs)
-
-    for j in range(3):
-        loads[j].wait()
-        if j == 2:
-            gather.q_along_y()
-
-        @pl.loop(0, 5)
-        def _(i):
-            cols = pl.ds(pl.multiple_of(j * D + i * 256, 256), 256)
-            part = matmul(normed[...], wqkv[:, cols]).astype(BF16)
-            if j > 0:
-                kv[:, pl.ds(pl.multiple_of((j - 1) * D + i * 256, 256), 256)] = part
-            projt[cols, :] = matmul_t(eye[...], part).astype(BF16)
-
+    project(1)
+    project(2)
+    gather.q_along_y()
     gather.p_along_y()
     same = ids_k == ids_q
 
@@ -532,7 +505,7 @@
             share = scores * (1.0 / jnp.sum(scores, axis=0, keepdims=True))
             probs[g * 8 + h] = share
             part = matmul(projt[pl.ds(2 * D + rows, 80), :], share.astype(BF16))
-            at[pl.ds(rows, 80), :] = part.astype(BF16)
+            at[pl.ds(rows, 80), pl.ds(0, 256)] = part.astype(BF16)
             gap = jnp.zeros((8, 256), F32)
             padded = jnp.concatenate([part[0:40], gap, part[40:80], gap], axis=0).astype(BF16)
             atp[pl.ds(pl.multiple_of(g * 768 + h * 96, 16), 96), :] = padded
@@ -541,26 +514,24 @@
     gather.q_along_x()
     attend(1)
     scatter = Scatter(
-        at, bg, dw_ref, (at2, bg2, wsum, wb, xa, yb, sa, sb, wa2, wb2, ya, xb, zs, zr, s3), ssem, norm_scale
+        at, bg, dw_ref, (pair, wsum, wb, xa, yb, sa, sb, wa2, wb2, ya, xb, zs, zr, s3), ssem, norm_scale
     )
     scatter.send_attended()
+
+    across = xp[...].T.astype(F32)
+    across = across - jnp.mean(across, axis=0, keepdims=True)
+    inv = lax.rsqrt(jnp.mean(across * across, axis=0, keepdims=True) + eps)
+    std[...] = across * inv
+    column = jnp.broadcast_to(gain_ref[...].reshape(1, D), (128, D)).T
+    gaincol[:, 0:128] = column
+    gaincol[:, 128:256] = column
+    apad[...] = atp[...].T
+    gather.p_pair()
     exchange_wait(cslab, crecv, csend, crecvs)
     bg[...] = crecv[...].reshape(256, D)
     scatter.send_grad()
-    gather.p_pair()
-    for j in range(6):
-        apad[:, pl.ds(j * 256, 256)] = matmul_t(eye[...], atp[pl.ds(j * 256, 256), :]).astype(BF16)
+    bgt[...] = bg[...].T
     scatter.product()
-
-
-    @pl.loop(0, 5)
-    def _(i):
-        rows = pl.ds(pl.multiple_of(i * 256, 256), 256)
-        total = jnp.zeros((256, 256), F32)
-        for part in three_parts(gain_ref[rows].reshape(1, 256)):
-            total += matmul_t(eye[...], jnp.broadcast_to(part, (256, 256)))
-        gaincol[rows, :] = total
-
     gather.q_pair()
     gather.finish()
     for half in range(2):
@@ -596,55 +567,30 @@
     back(0)
     scatter.after_one()
     back(1)
-    scatter.after_two()
-
-    def standard_of(i):
-        return matmul_t(eye[...], xp[:, pl.ds(pl.multiple_of(i * 256, 256), 256)])
-
-    def sums(i, carry):
-        return carry + jnp.sum(standard_of(i), axis=0, keepdims=True)
-
-    mean = lax.fori_loop(0, 5, sums, jnp.zeros((1, 256), F32)) * (1.0 / D)
-
-    def squares(i, carry):
-        part = standard_of(i) - mean
-        return carry + jnp.sum(part * part, axis=0, keepdims=True)
-
-    inv = lax.rsqrt(lax.fori_loop(0, 5, squares, jnp.zeros((1, 256), F32)) * (1.0 / D) + eps)
-
-    def grads(i, carry):
-        rows = pl.ds(pl.multiple_of(i * 256, 256), 256)
+
+    def grads(i):
+        rows = pl.ds(i * HALF, HALF)
         part = matmul(wqkv[rows, :], gt[...])
-        std = (standard_of(i) - mean) * inv
-        both = part * std
-        ones = jnp.ones((8, 256), BF16)
-        hi, mid, lo = three_parts(both)
-        row = matmul_t(ones, hi) + matmul_t(ones, mid) + matmul_t(ones, lo)
-        ghold[2, :, rows] = row[0:1]
+        both = part * std[rows, :]
+        both = both[:, 0:128] + both[:, 128:256]
+        ghold[2, :, rows] = jnp.sum(both.T, axis=0, keepdims=True)
         scaled = part * gaincol[rows, :]
         gn[rows, :] = scaled
-        a, b = carry
-        return (a + jnp.sum(scaled, axis=0, keepdims=True), b + jnp.sum(scaled * std, axis=0, keepdims=True))
-
-    zero = jnp.zeros((1, 256), F32)
-    mean_g, mean_gs = lax.fori_loop(0, 5, grads, (zero, zero))
+        return jnp.sum(scaled, axis=0, keepdims=True), jnp.sum(scaled * std[rows, :], axis=0, keepdims=True)
+
+    low = grads(0)
+    scatter.after_two()
+    high = grads(1)
     gains = GainSum(ghold, g1, g2, gsem)
     gains.first(ghold[2])
+    mean_g = (low[0] + high[0]) * (1.0 / D)
+    mean_gs = (low[1] + high[1]) * (1.0 / D)
+    branch = inv * (gn[...] - mean_g - std[...] * mean_gs)
+    total = (bgt[...].astype(F32) + branch).astype(BF16)
+    gx_ref[...] = matmul_t(permt[...], total).astype(BF16)
     scatter.after_z()
-    mean_g = mean_g * (1.0 / D)
-    mean_gs = mean_gs * (1.0 / D)
-
-    @pl.loop(0, 5)
-    def _(i):
-        rows = pl.ds(pl.multiple_of(i * 256, 256), 256)
-        std = (standard_of(i) - mean) * inv
-        branch = inv * (gn[rows, :] - mean_g - std * mean_gs)
-        total = (matmul_t(eye[...], bg[:, rows]) + branch).astype(BF16)
-        gx_ref[:, rows] = matmul_t(permt[...], total).astype(BF16)
-
     gains.second()
     exchange_wait(tok, got, tsend, trecvs)
-
     dg_ref[...] = gains.finish() * norm_scale
     scatter.finish()
 
@@ -695,18 +641,17 @@
             pltpu.VMEM((256, 2 * D), BF16),
             pltpu.VMEM((3 * D, 256), BF16),
             pltpu.VMEM((256, 256), BF16),
-            pltpu.VMEM((256, 256), BF16),
-            pltpu.VMEM((256, 256), BF16),
             pltpu.VMEM((HEADS, 256, 256), F32),
-            pltpu.VMEM((D, 256), BF16),
+            pltpu.VMEM((D, 512), BF16),
             pltpu.VMEM((1536, 256), BF16),
             pltpu.VMEM((256, 1536), BF16),
             pltpu.VMEM((256, D), BF16),
             pltpu.VMEM((D, 256), BF16),
+            pltpu.VMEM((D, 256), BF16),
             pltpu.VMEM((3 * D, 256), BF16),
             pltpu.VMEM((D, 256), F32),
-            pltpu.VMEM((D, 256), BF16),
-            pltpu.VMEM((256, HALF), BF16),
+            pltpu.VMEM((D, 256), F32),
+            pltpu.VMEM((512, HALF), BF16),
             pltpu.VMEM((NX, NY, 80, HALF), F32),
             pltpu.VMEM((NX, NY, 80, HALF), BF16),
             pltpu.VMEM((3, NY, 80, 384), BF16),
@@ -725,12 +670,12 @@
             pltpu.VMEM((15, 1, D), F32),
             pltpu.VMEM((D, 256), F32),
             pltpu.SemaphoreType.DMA((3,)),
-            pltpu.SemaphoreType.DMA((50,)),
+            pltpu.SemaphoreType.DMA((80,)),
             pltpu.SemaphoreType.DMA,
             pltpu.SemaphoreType.DMA,
             pltpu.SemaphoreType.DMA,
             pltpu.SemaphoreType.DMA,
-            pltpu.SemaphoreType.DMA((47,)),
+            pltpu.SemaphoreType.DMA((72,)),
             pltpu.SemaphoreType.DMA((60,)),
         ],
         compiler_params=pltpu.CompilerParams(
@@ -749,7 +694,7 @@
         ),
         in_specs=[vmem] * 4,
         out_specs=(vmem,) * 4,
-        compiler_params=pltpu.CompilerParams(vmem_limit_bytes=2**24),
+        compiler_params=pltpu.CompilerParams(vmem_limit_bytes=LIMIT),
     )(got, gx, dw, dg)
     return (merged[None], gx[None], own_weight, own_gain)
 

time: 99.9 us -> 98.5 us (0.986)
  local copies, waits for them, and re-layouts: 3.77 us -> 0 us
  Pallas kernels: 95.2 us -> 97.7 us
    unnamed x8 -> x0, local copies, waits for them, and re-layouts: 3.77 us -> none
    pallas_call x1, Pallas kernels: 1.41 us -> 2.73 us  [per_device(): pl.pallas_call(finish_kernel, out_shape=(jax.ShapeDtypeStruct((SEQ, GROUP...]
    pallas_call x1, Pallas kernels: 93.8 us -> 95 us  [per_device(): pl.pallas_call(kernel, out_shape=(jax.ShapeDtypeStruct((SEQ, GROUP, D), B...]
where the time goes in v5:
time: 98.5 us; the launch traced here: 98.3 us
  Pallas kernels  97.7 us (99%)
    pallas_call x1, Pallas kernels, per_device(): pl.pallas_call(kernel, out_shape=(jax.ShapeDtypeStruct((SEQ, GROUP, D), B...  95 us
    pallas_call x1, Pallas kernels, per_device(): pl.pallas_call(finish_kernel, out_shape=(jax.ShapeDtypeStruct((SEQ, GROUP...  2.73 us

profile of v5, /device:TPU:1, one launch (start us, length us, event | category | flops | bytes accessed | tf_op | source)
XLA Modules:
  0.0 98.3 jit_solution(2390775209449224066)
XLA Ops:
  0.6 95.0 %shard_map.102 = (bf16[64,4,1280]{2,1,0:T(4,128)(2,1)}, bf16[256,1280]{1,0:T(8,128)(2,1)}, f32[2,2,16,640]{3,2,1,0:T(8,128)}, f32[1,1280]{1,0:T(1,128)}) custom-call(bf16[256,1280]{1,0:T(8,128)(2,1)} %bitcast.5, s32[1,64]{1,0:T(1,128)} %refs_1_.1, s32[1,4]{1,0:T(1,128)} %bitcast.7, f32[1280]{0:T(1024)} %refs_3_.1, bf16[1280,3840]{1,0:T(8,128)(2,1)} %refs_4_.1, ...), custom_call_target="tpu_custom_call" | custom-call | tf_op jit(solution)/shard_map/pallas_call | solution.py:622
  95.6 2.7 %shard_map.103 = (bf16[64,5120]{1,0:T(8,128)(2,1)}, bf16[256,1280]{1,0:T(8,128)(2,1)}, f32[20,1280]{1,0:T(8,128)}, f32[20]{0:T(128)}) custom-call(bf16[64,4,1280]{2,1,0:T(4,128)(2,1)} %get-tuple-element.12.got_ref, bf16[256,1280]{1,0:T(8,128)(2,1)} %get-tuple-element.13.gx_in, f32[2,2,16,640]{3,2,1,0:T(8,128)} %get-tuple-element.14.dw_ref, ...), custom_call_target="tpu_custom_call" | custom-call | tf_op jit(solution)/shard_map/pallas_call | solution.py:687

commit v6 on v5

--- a/solution.py
+++ b/solution.py
@@ -11,6 +11,8 @@
 GROUP = 4
 D = 1280
 HALF = 640
+PLAIN = 128
+X_FIRST = 384
 NZ, NY, NX = 8, 4, 4
 SEQ = 64
 LIMIT = 56 * 2**20
@@ -45,38 +47,47 @@
     )
 
 
+class Presence:
+    def __init__(self, news):
+        self.news = news
+
+    def signal(self, sem, seq, x):
+        pl.semaphore_signal(sem, inc=1, device_id=dev(seq, x), device_id_type=pl.DeviceIdType.MESH)
+
+    def greet(self):
+        seq, x, z, y, core = place()
+        barrier = pltpu.get_barrier_semaphore()
+        for k in range(1, NZ):
+            self.signal(barrier, seq_of(lax.rem(z + k, NZ), y, core), x)
+        for k in range(1, NY):
+            self.signal(barrier, seq_of(z, lax.rem(y + k, NY), core), x)
+        for k in range(1, NX):
+            self.signal(barrier, seq, lax.rem(x + k, NX))
+        self.signal(barrier, seq_of(z, y, 1 - core), x)
+
+    def lines(self):
+        seq, x, z, y, core = place()
+        pl.semaphore_wait(pltpu.get_barrier_semaphore(), 14)
+        for k in range(1, NY):
+            self.signal(self.news.at[0], seq_of(z, lax.rem(y + k, NY), core), x)
+
+    def half_plane(self):
+        seq, x, z, y, core = place()
+        pl.semaphore_wait(self.news.at[0], NY - 1)
+        self.signal(self.news.at[1], seq_of(z, y, 1 - core), x)
+
+    def plane(self):
+        seq, x, z, y, core = place()
+        pl.semaphore_wait(self.news.at[1], 1)
+        for k in range(1, NX):
+            self.signal(self.news.at[2], seq, lax.rem(x + k, NX))
+
+    def everybody(self):
+        pl.semaphore_wait(self.news.at[2], NX - 1)
+
+
 def owner_of(x, y, z):
     return 16 * x + 4 * y + lax.div(z, 2)
-
-
-def greet():
-    seq, x, z, y, core = place()
-    barrier = pltpu.get_barrier_semaphore()
-
-    def signal(to, where):
-        pl.semaphore_signal(barrier, inc=1, device_id=dev(to, where), device_id_type=pl.DeviceIdType.MESH)
-
-    @pl.loop(1, SEQ)
-    def _(k):
-        signal(lax.rem(seq + k, SEQ), x)
-
-    for kx in range(1, NX):
-        for ky in range(NY):
-            signal(seq_of(z, lax.rem(y + ky, NY), core), lax.rem(x + kx, NX))
-        signal(owner_of(x, y, z), lax.rem(x + kx, NX))
-
-    @pl.when(x != lax.div(seq, 16))
-    def _():
-        for part in range(2):
-            for other in range(2):
-                to = seq_of(2 * lax.rem(seq, 4) + part, lax.rem(lax.div(seq, 4), 4), other)
-                signal(to, lax.div(seq, 16))
-
-
-def all_here():
-    seq, x, z, y, core = place()
-    count = SEQ - 1 + 12 + 3 + jnp.where(x != lax.div(seq, 16), 4, 0)
-    pl.semaphore_wait(pltpu.get_barrier_semaphore(), count)
 
 
 def exchange_start(src, dst, send, recv):
@@ -135,7 +146,7 @@
     def __init__(self, w_ref, slots, wg, sems):
         self.w_ref, self.slots, self.wg = w_ref, slots, wg
         self.pool = Pool(sems)
-        self.p, self.q = pl.ds(0, 256), pl.ds(256, 384)
+        self.p, self.q = pl.ds(0, PLAIN), pl.ds(PLAIN, HALF - PLAIN)
 
     def send(self, part, to, x):
         one = remote(part, part, self.pool.take(), self.pool.take(), to, x)
@@ -161,14 +172,14 @@
         first = pl.multiple_of(core * HALF, 128)
         rows = jnp.concatenate([slots[0, :, pl.ds(first, HALF)], slots[1, :, pl.ds(first, HALF)]], axis=0)
         own = matmul(one_hot(48, 64, want), rows).astype(BF16)
-        wg[core, zh, zl, y, :, self.p] = own[:, 0:256]
+        wg[core, zh, zl, y, :, self.p] = own[:, 0:PLAIN]
         self.zsend = [self.pool.take() for _ in range(1, NZ)]
         both = self.pool.used
         self.zrecv = [self.pool.take() for _ in range(2)]
 
         @pl.when(zl == x)
         def _():
-            wg[core, zh, zl, y, :, self.q] = own[:, 256:640]
+            wg[core, zh, zl, y, :, self.q] = own[:, PLAIN:HALF]
             part = wg.at[core, zh, zl, y, :, self.q]
             for k in range(1, NZ):
                 to = seq_of(lax.rem(z + k, NZ), y, core)
@@ -246,7 +257,7 @@
         self.at_ref, self.bg_ref, self.out, self.bufs, self.sems = at_ref, bg_ref, out, bufs, sems
         self.pool = Pool(sems)
         self.norm_scale = norm_scale
-        self.a, self.b = pl.ds(0, 384), pl.ds(384, 256)
+        self.a, self.b = pl.ds(0, X_FIRST), pl.ds(X_FIRST, HALF - X_FIRST)
 
     def wait(self):
         for one in self.now:
@@ -429,7 +440,7 @@
      got, gx_ref, dw_ref, dg_ref,
      wqkv, slots, wg, cslab, crecv, tok, xp, normed, kv, projt, permt, probs, at, atp, apad, bg, bgt, dat, gt, gn, std, pair,
      wsum, wb, xa, yb, sa, sb, wa2, wb2, ya, xb, zs, zr, s3, ghold, g1, g2, gaincol,
-     wsem, asem, csend, crecvs, tsend, trecvs, ssem, gsem) = refs
+     wsem, news, asem, csend, crecvs, tsend, trecvs, ssem, gsem) = refs
     score_scale = 1.0 / math.sqrt(80)
 
     loads = []
@@ -439,7 +450,8 @@
     for one in loads:
         one.start()
 
-    greet()
+    presence = Presence(news)
+    presence.greet()
 
     def shuffle(r, c):
         return c == lax.rem(r, 4) * 64 + lax.div(r, 4)
@@ -472,7 +484,7 @@
     spread = lax.rsqrt(jnp.mean(centred * centred, axis=-1, keepdims=True) + eps)
     normed[...] = (centred * spread * gain_ref[...].reshape(1, D)).astype(BF16)
 
-    all_here()
+    presence.lines()
     gather = Gather(wout_ref, slots, wg, asem)
     gather.pair()
 
@@ -486,11 +498,13 @@
 
     project(0)
     gather.along_z()
-    exchange_start(cslab, crecv, csend, crecvs)
+    presence.half_plane()
     project(1)
     project(2)
+    presence.plane()
     gather.q_along_y()
     gather.p_along_y()
+    exchange_start(cslab, crecv, csend, crecvs)
     same = ids_k == ids_q
 
     def attend(g):
@@ -581,6 +595,7 @@
     low = grads(0)
     scatter.after_two()
     high = grads(1)
+    presence.everybody()
     gains = GainSum(ghold, g1, g2, gsem)
     gains.first(ghold[2])
     mean_g = (low[0] + high[0]) * (1.0 / D)
@@ -654,14 +669,14 @@
             pltpu.VMEM((512, HALF), BF16),
             pltpu.VMEM((NX, NY, 80, HALF), F32),
             pltpu.VMEM((NX, NY, 80, HALF), BF16),
-            pltpu.VMEM((3, NY, 80, 384), BF16),
-            pltpu.VMEM((3, NX, 80, 256), BF16),
-            pltpu.VMEM((NY, 80, 384), F32),
-            pltpu.VMEM((NX, 80, 256), F32),
-            pltpu.VMEM((NY, 80, 384), BF16),
-            pltpu.VMEM((NX, 80, 256), BF16),
-            pltpu.VMEM((3, 80, 384), BF16),
-            pltpu.VMEM((3, 80, 256), BF16),
+            pltpu.VMEM((3, NY, 80, X_FIRST), BF16),
+            pltpu.VMEM((3, NX, 80, HALF - X_FIRST), BF16),
+            pltpu.VMEM((NY, 80, X_FIRST), F32),
+            pltpu.VMEM((NX, 80, HALF - X_FIRST), F32),
+            pltpu.VMEM((NY, 80, X_FIRST), BF16),
+            pltpu.VMEM((NX, 80, HALF - X_FIRST), BF16),
+            pltpu.VMEM((3, 80, X_FIRST), BF16),
+            pltpu.VMEM((3, 80, HALF - X_FIRST), BF16),
             pltpu.VMEM((128, HALF), BF16),
             pltpu.VMEM((7, 16, HALF), BF16),
             pltpu.VMEM((16, HALF), F32),
@@ -670,6 +685,7 @@
             pltpu.VMEM((15, 1, D), F32),
             pltpu.VMEM((D, 256), F32),
             pltpu.SemaphoreType.DMA((3,)),
+            pltpu.SemaphoreType.REGULAR((3,)),
             pltpu.SemaphoreType.DMA((80,)),
             pltpu.SemaphoreType.DMA,
             pltpu.SemaphoreType.DMA,

time: 98.5 us -> 94.5 us (0.959)
  Pallas kernels: 97.7 us -> 93.8 us
    pallas_call x1, Pallas kernels: 95 us -> 91 us  [per_device(): pl.pallas_call(kernel, out_shape=(jax.ShapeDtypeStruct((SEQ, GROUP, D), B...]
where the time goes in v6:
time: 94.5 us; the launch traced here: 94.4 us
  Pallas kernels  93.8 us (99%)
    pallas_call x1, Pallas kernels, per_device(): pl.pallas_call(kernel, out_shape=(jax.ShapeDtypeStruct((SEQ, GROUP, D), B...  91 us
    pallas_call x1, Pallas kernels, per_device(): pl.pallas_call(finish_kernel, out_shape=(jax.ShapeDtypeStruct((SEQ, GROUP...  2.73 us

profile of v6, /device:TPU:1, one launch (start us, length us, event | category | flops | bytes accessed | tf_op | source)
XLA Modules:
  0.0 94.4 jit_solution(15306340308099978661)
XLA Ops:
  0.6 91.0 %shard_map.102 = (bf16[64,4,1280]{2,1,0:T(4,128)(2,1)}, bf16[256,1280]{1,0:T(8,128)(2,1)}, f32[2,2,16,640]{3,2,1,0:T(8,128)}, f32[1,1280]{1,0:T(1,128)}) custom-call(bf16[256,1280]{1,0:T(8,128)(2,1)} %bitcast.5, s32[1,64]{1,0:T(1,128)} %refs_1_.1, s32[1,4]{1,0:T(1,128)} %bitcast.7, f32[1280]{0:T(1024)} %refs_3_.1, bf16[1280,3840]{1,0:T(8,128)(2,1)} %refs_4_.1, ...), custom_call_target="tpu_custom_call" | custom-call | tf_op jit(solution)/shard_map/pallas_call | solution.py:637
  91.7 2.7 %shard_map.103 = (bf16[64,5120]{1,0:T(8,128)(2,1)}, bf16[256,1280]{1,0:T(8,128)(2,1)}, f32[20,1280]{1,0:T(8,128)}, f32[20]{0:T(128)}) custom-call(bf16[64,4,1280]{2,1,0:T(4,128)(2,1)} %get-tuple-element.12.got_ref, bf16[256,1280]{1,0:T(8,128)(2,1)} %get-tuple-element.13.gx_in, f32[2,2,16,640]{3,2,1,0:T(8,128)} %get-tuple-element.14.dw_ref, ...), custom_call_target="tpu_custom_call" | custom-call | tf_op jit(solution)/shard_map/pallas_call | solution.py:703

commit v7 on v6

--- a/solution.py
+++ b/solution.py
@@ -86,8 +86,13 @@
         pl.semaphore_wait(self.news.at[2], NX - 1)
 
 
+def piece_of(x, z):
+    return lax.rem(z - 2 * x + 3 + NZ, NZ)
+
+
 def owner_of(x, y, z):
-    return 16 * x + 4 * y + lax.div(z, 2)
+    piece = piece_of(x, z)
+    return seq_of(2 * x + lax.div(piece, 4), y, lax.rem(lax.div(piece, 2), 2))
 
 
 def exchange_start(src, dst, send, recv):
@@ -289,9 +294,11 @@
         for k in (1, 2, 3, 0):
             i = lax.rem(x + k, NX)
             rows = pl.ds(pl.multiple_of(i * 320, 64), 320)
-            part = matmul(self.at_ref[rows, :], pair[...]).reshape(NY, 80, HALF)
-            wsum[i] = part
-            wb[i] = part.astype(BF16)
+            part = matmul(self.at_ref[rows, :], pair[...]).reshape(2, NY, 40, HALF)
+            for j in range(NY):
+                own = jnp.concatenate([part[0, j], part[1, j]], axis=0)
+                wsum[i, j] = own
+                wb[i, j] = own.astype(BF16)
             if k > 0:
                 self.now.append(self.send(wb.at[i, :, :, self.a], xa.at[k - 1], seq, i))
             for j in range(1, NY):
@@ -344,7 +351,7 @@
         self.now = []
         for k in range(1, NZ):
             to = lax.rem(z + k, NZ)
-            src = zs.at[pl.ds(pl.multiple_of(to * 16, 16), 16)]
+            src = zs.at[pl.ds(pl.multiple_of(piece_of(x, to) * 16, 16), 16)]
             self.now.append(self.send(src, zr.at[k - 1], seq_of(to, y, core), x))
 
     def after_z(self):
@@ -352,12 +359,12 @@
         seq, x, z, y, core = place()
         out = self.out
         self.wait()
-        total = zs[pl.ds(pl.multiple_of(z * 16, 16), 16), :].astype(F32)
+        total = zs[pl.ds(pl.multiple_of(piece_of(x, z) * 16, 16), 16), :].astype(F32)
         for k in range(7):
             total += zr[k].astype(F32)
-        s3[...] = total * self.norm_scale
+        s3[...] = (total * self.norm_scale).astype(BF16)
         owner = owner_of(x, y, z)
-        slot = out.at[lax.rem(z, 2), core]
+        slot = out.at[lax.rem(piece_of(x, z), 2), core]
         self.sent, self.got = self.pool.take(), self.pool.take()
         self.now = [
             remote(s3, slot, self.pool.take(), self.got, owner, lax.rem(x + k, NX)) for k in range(1, NX)
@@ -436,13 +443,20 @@
 
 
 def kernel_body(norm_scale, refs):
-    (x_ref, dest_ref, len_ref, gain_ref, wqkv_hbm, wout_ref, cot_ref,
+    (x_hbm, dest_ref, len_ref, gain_ref, wqkv_hbm, wout_hbm, cot_hbm,
      got, gx_ref, dw_ref, dg_ref,
-     wqkv, slots, wg, cslab, crecv, tok, xp, normed, kv, projt, permt, probs, at, atp, apad, bg, bgt, dat, gt, gn, std, pair,
+     x_ref, wout_ref, cot_ref, wqkv, slots, wg, cslab, crecv, tok, xp, normed, kv, projt, permt, probs, at, atp, apad, bg, bgt, dat, gt, gn, std, pair,
      wsum, wb, xa, yb, sa, sb, wa2, wb2, ya, xb, zs, zr, s3, ghold, g1, g2, gaincol,
      wsem, news, asem, csend, crecvs, tsend, trecvs, ssem, gsem) = refs
     score_scale = 1.0 / math.sqrt(80)
 
+    cot_load = pltpu.make_async_copy(cot_hbm, cot_ref, wsem.at[3])
+    x_load = pltpu.make_async_copy(x_hbm, x_ref, wsem.at[4])
+    out_load = pltpu.make_async_copy(wout_hbm, wout_ref, wsem.at[5])
+    for one in (cot_load, out_load, x_load):
+        one.start()
+    presence = Presence(news)
+    presence.greet()
     loads = []
     for j in range(3):
         cols = pl.ds(j * D, D)
@@ -450,12 +464,10 @@
     for one in loads:
         one.start()
 
-    presence = Presence(news)
-    presence.greet()
-
     def shuffle(r, c):
         return c == lax.rem(r, 4) * 64 + lax.div(r, 4)
 
+    cot_load.wait()
     stacked = jnp.concatenate([cot_ref[:, pl.ds(c * D, D)] for c in range(4)], axis=0)
     cslab[...] = matmul(one_hot(256, 256, shuffle), stacked).astype(BF16).reshape(SEQ, GROUP, D)
     slot = jnp.broadcast_to(lax.shift_right_logical(dest_ref[...], 6), (8, 64)).astype(F32).astype(BF16)
@@ -478,6 +490,8 @@
     ids_k = jnp.sum(jnp.where(ir == key_row, id_row, 0.0), axis=1, keepdims=True)
     ids_q = jnp.sum(jnp.where(ic == key_col, id_col, 0.0), axis=0, keepdims=True)
 
+    x_load.wait()
+    out_load.wait()
     wide = matmul(perm, x_ref[...])
     xp[...] = wide.astype(BF16)
     centred = wide - jnp.mean(wide, axis=-1, keepdims=True)
@@ -619,7 +633,8 @@
     gx_ref[...] = gx_in[...]
     for part in range(2):
         for core in range(2):
-            own_ref[pl.ds(10 * part, 10), pl.ds(core * HALF, HALF)] = dw_ref[part, core, 0:10, :]
+            own = dw_ref[part, core].astype(F32)
+            own_ref[pl.ds(10 * part, 10), pl.ds(core * HALF, HALF)] = own[0:10]
     first = lax.axis_index("seq") * 20
     turned = pltpu.roll(jnp.broadcast_to(dg_ref[...], (8, D)), lax.rem(D - first, D), 1)
     gain_out[...] = turned[0, 0:20]
@@ -639,12 +654,15 @@
         out_shape=(
             jax.ShapeDtypeStruct((SEQ, GROUP, D), BF16),
             jax.ShapeDtypeStruct((256, D), BF16),
-            jax.ShapeDtypeStruct((2, 2, 16, HALF), F32),
+            jax.ShapeDtypeStruct((2, 2, 16, HALF), BF16),
             jax.ShapeDtypeStruct((1, D), F32),
         ),
-        in_specs=[vmem, vmem, smem, vmem, hbm, vmem, vmem],
-        out_specs=(vmem,) * 4,
+        in_specs=[hbm, vmem, smem, vmem, hbm, hbm, hbm],
+        out_specs=(hbm, vmem, vmem, vmem),
         scratch_shapes=[
+            pltpu.VMEM((256, D), BF16),
+            pltpu.VMEM((20, D), BF16),
+            pltpu.VMEM((SEQ, GROUP * D), BF16),
             pltpu.VMEM((D, 3 * D), BF16),
             pltpu.VMEM((2, 32, D), BF16),
             pltpu.VMEM((2, 2, 4, NY, 48, HALF), BF16),
@@ -679,12 +697,12 @@
             pltpu.VMEM((3, 80, HALF - X_FIRST), BF16),
             pltpu.VMEM((128, HALF), BF16),
             pltpu.VMEM((7, 16, HALF), BF16),
-            pltpu.VMEM((16, HALF), F32),
+            pltpu.VMEM((16, HALF), BF16),
             pltpu.VMEM((3, 1, D), F32),
             pltpu.VMEM((15, 1, D), F32),
             pltpu.VMEM((15, 1, D), F32),
             pltpu.VMEM((D, 256), F32),
-            pltpu.SemaphoreType.DMA((3,)),
+            pltpu.SemaphoreType.DMA((6,)),
             pltpu.SemaphoreType.REGULAR((3,)),
             pltpu.SemaphoreType.DMA((80,)),
             pltpu.SemaphoreType.DMA,

time: 94.5 us -> 84.9 us (0.90)
  Pallas kernels: 93.8 us -> 84.1 us
    pallas_call x1, Pallas kernels: 91 us -> 81.4 us  [per_device(): pl.pallas_call(kernel, out_shape=(jax.ShapeDtypeStruct((SEQ, GROUP, D), B...]
where the time goes in v7:
time: 84.9 us; the launch traced here: 84.7 us
  Pallas kernels  84.1 us (99%)
    pallas_call x1, Pallas kernels, per_device(): pl.pallas_call(kernel, out_shape=(jax.ShapeDtypeStruct((SEQ, GROUP, D), B...  81.4 us
    pallas_call x1, Pallas kernels, per_device(): pl.pallas_call(finish_kernel, out_shape=(jax.ShapeDtypeStruct((SEQ, GROUP...  2.71 us

profile of v7, /device:TPU:1, one launch (start us, length us, event | category | flops | bytes accessed | tf_op | source)
XLA Modules:
  0.0 84.7 jit_solution(1285393655610438823)
XLA Ops:
  0.6 81.4 %shard_map.102 = (bf16[64,4,1280]{2,1,0:T(4,128)(2,1)}, bf16[256,1280]{1,0:T(8,128)(2,1)}, bf16[2,2,16,640]{3,2,1,0:T(8,128)(2,1)}, f32[1,1280]{1,0:T(1,128)}) custom-call(bf16[256,1280]{1,0:T(8,128)(2,1)} %bitcast.5, s32[1,64]{1,0:T(1,128)} %refs_1_.1, s32[1,4]{1,0:T(1,128)} %bitcast.7, f32[1280]{0:T(1024)} %refs_3_.1, bf16[1280,3840]{1,0:T(8,128)(2,1)} %refs_4_.1, ...), custom_call_target="tpu_custom_call" | custom-call | tf_op jit(solution)/shard_map/pallas_call | solution.py:652
  82.0 2.7 %shard_map.103 = (bf16[64,5120]{1,0:T(8,128)(2,1)}, bf16[256,1280]{1,0:T(8,128)(2,1)}, f32[20,1280]{1,0:T(8,128)}, f32[20]{0:T(128)}) custom-call(bf16[64,4,1280]{2,1,0:T(4,128)(2,1)} %get-tuple-element.12.got_ref, bf16[256,1280]{1,0:T(8,128)(2,1)} %get-tuple-element.13.gx_in, bf16[2,2,16,640]{3,2,1,0:T(8,128)(2,1)} %get-tuple-element.14.dw_ref, ...), custom_call_target="tpu_custom_call" | custom-call | tf_op jit(solution)/shard_map/pallas_call | solution.py:721

commit v8 on v7

--- a/solution.py
+++ b/solution.py
@@ -593,8 +593,8 @@
             gt[pl.ds(2 * D + rows, 80), :] = matmul_t(dat[pl.ds(rows, 80), :], low).astype(BF16)
 
     back(0)
+    back(1)
     scatter.after_one()
-    back(1)
 
     def grads(i):
         rows = pl.ds(i * HALF, HALF)
@@ -607,18 +607,18 @@
         return jnp.sum(scaled, axis=0, keepdims=True), jnp.sum(scaled * std[rows, :], axis=0, keepdims=True)
 
     low = grads(0)
-    scatter.after_two()
     high = grads(1)
     presence.everybody()
     gains = GainSum(ghold, g1, g2, gsem)
     gains.first(ghold[2])
+    scatter.after_two()
     mean_g = (low[0] + high[0]) * (1.0 / D)
     mean_gs = (low[1] + high[1]) * (1.0 / D)
     branch = inv * (gn[...] - mean_g - std[...] * mean_gs)
     total = (bgt[...].astype(F32) + branch).astype(BF16)
     gx_ref[...] = matmul_t(permt[...], total).astype(BF16)
+    gains.second()
     scatter.after_z()
-    gains.second()
     exchange_wait(tok, got, tsend, trecvs)
     dg_ref[...] = gains.finish() * norm_scale
     scatter.finish()

time: 84.9 us -> 83.5 us (0.984)
  the two profiles are of different devices: /device:TPU:1 before, /device:TPU:6 now
where the time goes in v8:
time: 83.5 us; the launch traced here: 83.3 us
  Pallas kernels  82.7 us (99%)
    pallas_call x1, Pallas kernels, per_device(): pl.pallas_call(kernel, out_shape=(jax.ShapeDtypeStruct((SEQ, GROUP, D), B...  80 us
    pallas_call x1, Pallas kernels, per_device(): pl.pallas_call(finish_kernel, out_shape=(jax.ShapeDtypeStruct((SEQ, GROUP...  2.71 us

profile of v8, /device:TPU:6, one launch (start us, length us, event | category | flops | bytes accessed | tf_op | source)
XLA Modules:
  0.0 83.3 jit_solution(5264455549509864934)
XLA Ops:
  0.6 80.0 %shard_map.102 = (bf16[64,4,1280]{2,1,0:T(4,128)(2,1)}, bf16[256,1280]{1,0:T(8,128)(2,1)}, bf16[2,2,16,640]{3,2,1,0:T(8,128)(2,1)}, f32[1,1280]{1,0:T(1,128)}) custom-call(bf16[256,1280]{1,0:T(8,128)(2,1)} %bitcast.5, s32[1,64]{1,0:T(1,128)} %refs_1_.1, s32[1,4]{1,0:T(1,128)} %bitcast.7, f32[1280]{0:T(1024)} %refs_3_.1, bf16[1280,3840]{1,0:T(8,128)(2,1)} %refs_4_.1, ...), custom_call_target="tpu_custom_call" | custom-call | tf_op jit(solution)/shard_map/pallas_call | solution.py:652
  80.6 2.7 %shard_map.103 = (bf16[64,5120]{1,0:T(8,128)(2,1)}, bf16[256,1280]{1,0:T(8,128)(2,1)}, f32[20,1280]{1,0:T(8,128)}, f32[20]{0:T(128)}) custom-call(bf16[64,4,1280]{2,1,0:T(4,128)(2,1)} %get-tuple-element.12.got_ref, bf16[256,1280]{1,0:T(8,128)(2,1)} %get-tuple-element.13.gx_in, bf16[2,2,16,640]{3,2,1,0:T(8,128)(2,1)} %get-tuple-element.14.dw_ref, ...), custom_call_target="tpu_custom_call" | custom-call | tf_op jit(solution)/shard_map/pallas_call | solution.py:721

commit v9 on v8

--- a/solution.py
+++ b/solution.py
@@ -97,12 +97,11 @@
 
 def exchange_start(src, dst, send, recv):
     seq, x, z, y, core = place()
-
-    @pl.loop(1, SEQ)
-    def _(k):
-        to = lax.rem(seq + k, SEQ)
+    ways = [(kz, ky, kc) for kz in range(NZ) for ky in range(NY) for kc in range(2)][1:]
+    ways.sort(key=lambda way: -min(way[0], NZ - way[0]) - min(way[1], NY - way[1]))
+    for kz, ky, kc in ways:
+        to = seq_of(lax.rem(z + kz, NZ), lax.rem(y + ky, NY), lax.rem(core + kc, 2))
         remote(src.at[to], dst.at[seq], send, recv, to, x).start()
-
     pltpu.make_async_copy(src.at[seq], dst.at[seq], recv).start()
 
 

time: 83.5 us -> 82.5 us (0.988)
  the two profiles are of different devices: /device:TPU:6 before, /device:TPU:1 now
where the time goes in v9:
time: 82.5 us; the launch traced here: 82.3 us
  Pallas kernels  81.7 us (99%)
    pallas_call x1, Pallas kernels, per_device(): pl.pallas_call(kernel, out_shape=(jax.ShapeDtypeStruct((SEQ, GROUP, D), B...  79 us
    pallas_call x1, Pallas kernels, per_device(): pl.pallas_call(finish_kernel, out_shape=(jax.ShapeDtypeStruct((SEQ, GROUP...  2.71 us

profile of v9, /device:TPU:1, one launch (start us, length us, event | category | flops | bytes accessed | tf_op | source)
XLA Modules:
  0.0 82.3 jit_solution(9246331387155528518)
XLA Ops:
  0.6 79.0 %shard_map.102 = (bf16[64,4,1280]{2,1,0:T(4,128)(2,1)}, bf16[256,1280]{1,0:T(8,128)(2,1)}, bf16[2,2,16,640]{3,2,1,0:T(8,128)(2,1)}, f32[1,1280]{1,0:T(1,128)}) custom-call(bf16[256,1280]{1,0:T(8,128)(2,1)} %bitcast.5, s32[1,64]{1,0:T(1,128)} %refs_1_.1, s32[1,4]{1,0:T(1,128)} %bitcast.7, f32[1280]{0:T(1024)} %refs_3_.1, bf16[1280,3840]{1,0:T(8,128)(2,1)} %refs_4_.1, ...), custom_call_target="tpu_custom_call" | custom-call | tf_op jit(solution)/shard_map/pallas_call | solution.py:651
  79.6 2.7 %shard_map.103 = (bf16[64,5120]{1,0:T(8,128)(2,1)}, bf16[256,1280]{1,0:T(8,128)(2,1)}, f32[20,1280]{1,0:T(8,128)}, f32[20]{0:T(128)}) custom-call(bf16[64,4,1280]{2,1,0:T(4,128)(2,1)} %get-tuple-element.12.got_ref, bf16[256,1280]{1,0:T(8,128)(2,1)} %get-tuple-element.13.gx_in, bf16[2,2,16,640]{3,2,1,0:T(8,128)(2,1)} %get-tuple-element.14.dw_ref, ...), custom_call_target="tpu_custom_call" | custom-call | tf_op jit(solution)/shard_map/pallas_call | solution.py:720
